TPU v7x, 512 devices: a whole 4x8x8 slice. The times are simulated.
512 devices in a mesh: outer: 32 (over z, x_hi, core), chip: 16 (over y, x_lo).
Axes of the slice: x: 4 (x_hi: 2, x_lo: 2; x = x_hi * 2 + x_lo), y: 8, z: 8, core: 2. Of those that a mesh axis runs over, the one named last changes fastest.
Arguments:
- hidden: bfloat16 [64, 256, 2048], P('outer', 'chip'), may hold values from -6 to 6
- down_weight: bfloat16 [64, 2048, 7168], P('outer', None, 'chip'), may hold values from -0.125 to 0.125
- out_grad: bfloat16 [1536, 7168], P('outer', 'chip'), may hold values from -6 to 6
- routes: int32 [1536, 8], P('outer'), may hold values from 0 to 63, as said below
- gates: float32 [1536, 8], P('outer'), may hold values from 0.1 to 0.6
- omega: float32 [7168, 32], P('chip'), may hold values from -0.0625 to 0.0625
- psi: float32 [2048, 32], replicated, may hold values from -0.125 to 0.125
- left_old: float32 [64, 2048, 32], P('outer', 'chip'), may hold values from -6 to 6
- right_old: float32 [64, 7168, 32], P('outer', 'chip'), may hold values from -6 to 6
- moves: int32 [4, 2], replicated, may hold values from 0 to 31, as said below
Outputs:
- mixed: bfloat16 [1536, 7168], P('outer', 'chip')
- hidden_grad: bfloat16 [64, 256, 2048], P('outer', 'chip')
- left_moved: float32 [64, 2048, 32], P('outer', 'chip')
- right_moved: float32 [64, 7168, 32], P('outer', 'chip')
Inputs may be any that keep to these rules, and one draw needn't show every extreme that they name: `routes`: each row names 8 different experts, all of them in at most 4 pods, where pod q holds the experts 2 * 2 * q to 2 * 2 * (q + 1) - 1. `moves`: the 8 entries are different groups. In some row the two groups are 16 apart, and in some other row they are neighbours (index difference 1).
All inputs are finite; a program needn't handle non-finite values.
Results may differ from a plain program's by a relative error of at most 0.022.
Values may be sent and summed in bfloat16 or wider, within the bound.
A program may use at most 64 MiB of HBM per device.

v0:
```python
import math

import jax
import jax.numpy as jnp
from jax import lax
from jax.sharding import PartitionSpec as P

highest = lax.Precision.HIGHEST


def broadcast(shard, axis, root):
    mine = lax.axis_index(axis) == root
    return lax.psum(jnp.where(mine, shard, jnp.zeros_like(shard)), axis)


def on_device(hidden, down_weight, out_grad, routes, gates, omega, psi, left_old, right_old, moves):
    outer_size = lax.axis_size("outer")
    chip_size = lax.axis_size("chip")
    local_experts = down_weight.shape[0]
    hidden_width = down_weight.shape[1]
    column_count = down_weight.shape[2]
    model_width = column_count * chip_size
    token_rows = routes.shape[0]
    pick_count = routes.shape[1]
    expert_rows = hidden.shape[1] * chip_size
    slot_count = expert_rows // outer_size
    all_experts = local_experts * outer_size
    buffer_rows = all_experts * slot_count
    pair_ids = routes.reshape(-1)
    onehot = (pair_ids[:, None] == jnp.arange(all_experts, dtype=jnp.int32)[None, :]).astype(
        jnp.int32
    )
    earlier = jnp.cumsum(onehot, axis=0) - onehot
    rank_of = jnp.sum(earlier * onehot, axis=1)
    local_index = pair_ids % local_experts
    group_index = pair_ids // local_experts
    buffer_index = local_index * expert_rows + group_index * slot_count + rank_of
    buffer_index = jnp.where(rank_of < slot_count, buffer_index, -1)
    matches = (buffer_index[:, None] == jnp.arange(buffer_rows, dtype=jnp.int32)[None, :]).astype(
        jnp.float32
    )
    weighted = matches * gates.reshape(-1)[:, None]
    assign = jnp.sum(weighted.reshape(token_rows, pick_count, buffer_rows), axis=1)
    outgoing = jnp.dot(assign.T, out_grad.astype(jnp.float32), precision=highest).astype(
        jnp.bfloat16
    )
    outgoing = outgoing.reshape(local_experts, outer_size, slot_count, column_count)
    expert_grad = lax.all_to_all(
        outgoing, "outer", split_axis=1, concat_axis=1, tiled=True
    ).reshape(local_experts, expert_rows, column_count)
    full_rows = lax.all_gather(hidden, "chip", axis=1, tiled=True)
    expert_out = jnp.einsum(
        "kmf,kfd->kmd", full_rows, down_weight, preferred_element_type=jnp.float32
    ).astype(jnp.bfloat16)
    returned = lax.all_to_all(
        expert_out.reshape(local_experts, outer_size, slot_count, column_count),
        "outer",
        split_axis=1,
        concat_axis=1,
        tiled=True,
    )
    mixed = jnp.dot(
        assign, returned.reshape(buffer_rows, column_count).astype(jnp.float32), precision=highest
    ).astype(jnp.bfloat16)
    partial_value = jnp.einsum(
        "kmd,kfd->kmf", expert_grad, down_weight, preferred_element_type=jnp.float32
    )
    hidden_grad = lax.psum_scatter(
        partial_value.astype(jnp.bfloat16), "chip", scatter_dimension=1, tiled=True
    )
    scale_right = 10.0 / (
        expert_rows * (hidden_width / math.sqrt(model_width) + math.sqrt(hidden_width))
    )
    scale_left = 10.0 / (
        expert_rows * (model_width / math.sqrt(hidden_width) + math.sqrt(model_width))
    )
    weight_grad = jnp.einsum(
        "kmf,kmd->kfd", full_rows, expert_grad, preferred_element_type=jnp.float32
    )
    cols_part = jnp.einsum("kfd,dr->kfr", weight_grad, omega, precision=highest)
    sketch_cols = lax.psum(cols_part.astype(jnp.bfloat16), "chip").astype(jnp.float32)
    right_step = jnp.einsum("kfd,kfr->kdr", weight_grad, sketch_cols, precision=highest)
    width_side = jnp.einsum("kfd,fr->kdr", weight_grad, psi, precision=highest)
    rows_part = jnp.einsum("kfd,kdr->kfr", weight_grad, width_side, precision=highest)
    left_step = lax.psum_scatter(
        rows_part.astype(jnp.bfloat16), "chip", scatter_dimension=1, tiled=True
    ).astype(jnp.float32)
    right_new = 0.5 * right_old + 0.5 * scale_right * right_step
    left_new = 0.5 * left_old + 0.5 * scale_left * left_step
    outer_index = lax.axis_index("outer")

    def fetch(payload, root_group):
        return (
            broadcast(payload[0].astype(jnp.bfloat16), "outer", root_group).astype(jnp.float32),
            broadcast(payload[1].astype(jnp.bfloat16), "outer", root_group).astype(jnp.float32),
        )

    left_moved, right_moved = (left_new, right_new)
    for move_index in range(moves.shape[0]):
        from_group = moves[move_index, 0]
        to_group = moves[move_index, 1]
        from_left, from_right = fetch((left_new, right_new), from_group)
        to_left, to_right = fetch((left_new, right_new), to_group)
        left_moved = jnp.where(
            outer_index == to_group,
            from_left,
            jnp.where(outer_index == from_group, to_left, left_moved),
        )
        right_moved = jnp.where(
            outer_index == to_group,
            from_right,
            jnp.where(outer_index == from_group, to_right, right_moved),
        )
    return (mixed, hidden_grad, left_moved, right_moved)


def solution(mesh):
    in_specs = (
        P("outer", "chip", None),
        P("outer", None, "chip"),
        P("outer", "chip"),
        P("outer", None),
        P("outer", None),
        P("chip", None),
        P(),
        P("outer", "chip", None),
        P("outer", "chip", None),
        P(),
    )
    out_specs = (
        P("outer", "chip"),
        P("outer", "chip", None),
        P("outer", "chip", None),
        P("outer", "chip", None),
    )
    return jax.shard_map(
        on_device, mesh=mesh, in_specs=in_specs, out_specs=out_specs, check_vma=False
    )
```

profile of v0, /device:TPU:1, one launch (start us, length us, event | category | flops | bytes accessed | tf_op | source)
XLA Modules:
  0.0 679.7 jit_solution(7644280688599719740)
XLA Ops:
  7.2 0.0 copy-start
  7.2 0.0 copy-start.6
  7.2 0.0 all-gather.2.cloned.1.call-start
  7.2 0.7 all-gather.2.cloned.1.call-update
  7.9 0.8 copy.45
  8.7 0.1 eq.47
  8.8 0.1 eq.43
  8.9 0.8 copy.52
  9.7 0.9 reduce-window.6
  10.6 0.2 slice_reduce_fusion
  10.8 0.1 fusion.16
  10.9 0.1 reduce_sum.21
  11.1 0.3 select_reduce_fusion
  11.4 1.4 convolution_convert_fusion.3
  12.8 0.2 copy.56
  13.0 0.9 copy.57
  13.8 14.4 %all-to-all-start.1 = ((bf16[2,32,8,448]{3,2,0,1:T(8,128)(2,1)}), bf16[2,32,8,448]{3,2,0,1:T(8,128)(2,1)S(1)}, u32[]{:S(2)}, u32[]{:S(2)}) async-start(bf16[2,32,8,448]{3,2,0,1:T(8,128)(2,1)} %copy.57), calls=%async_computation.1 | async-start | bytes 1048576 | tf_op jit(solution)/shard_map/all_to_all | solution.py:48
  28.3 0.0 all-reduce.4.cloned.1.call-start
  28.4 0.0 copy-done.6
  28.4 0.7 fusion.30
  34.2 11.1 %all-to-all-done.1 = bf16[2,32,8,448]{3,2,0,1:T(8,128)(2,1)S(1)} async-done(((bf16[2,32,8,448]{3,2,0,1:T(8,128)(2,1)}), bf16[2,32,8,448]{3,2,0,1:T(8,128)(2,1)S(1)}, u32[]{:S(2)}, u32[]{:S(2)}) %all-to-all-start.1) | async-done | bytes 458784 | tf_op jit(solution)/shard_map/all_to_all | solution.py:48
  45.3 40.4 %all-gather.2.cloned.1.call-done = bf16[2,256,2048]{2,1,0:T(8,128)(2,1)} async-done(((bf16[2,16,2048]{2,1,0:T(8,128)(2,1)}), bf16[2,256,2048]{2,1,0:T(8,128)(2,1)}) %all-gather.2.cloned.1.call-update) | async-done | bytes 2097168 | tf_op jit(solution)/shard_map/all_gather | solution.py:51
  85.7 2.7 fusion.8
  88.4 0.0 copy-done
  88.4 0.0 copy-start.1
  88.4 0.0 copy-start.5
  88.5 6.5 fusion.2
  94.9 0.0 copy-done.1
  94.9 0.0 copy-done.5
  94.9 5.2 fusion.4
  100.1 0.0 all-reduce.4.cloned.1.call-update
  100.1 0.0 copy-start.3
  100.1 0.2 reduce-scatter.7.cloned.1.call-start
  100.4 7.4 %convolution_convert_fusion.1 = bf16[2,2048,32]{1,2,0:T(8,128)(2,1)S(1)} fusion(f32[2,448,2048]{2,1,0:T(8,128)} %copy-done.1, f32[2,448,32]{1,2,0:T(8,128)S(1)} %fusion.2), kind=kOutput, calls=%fused_computation.6 | convolution fusion | flops 704774144 | bytes 7716864 | tf_op jit(solution)/shard_map/kfd,kdr->kfr/dot_general | solution.py:84
  107.8 0.7 copy.63
  108.5 1.3 reshape.110
  109.8 0.0 reduce-scatter.7.cloned.1.call-update
  109.8 0.0 copy-start.4
  109.8 0.0 all-reduce.6.cloned.1.call-start
  109.9 130.8 %all-reduce.4.cloned.1.call-done = bf16[2,2048,32]{1,2,0:T(8,128)(2,1)} async-done(((bf16[2,2048,32]{1,2,0:T(8,128)(2,1)}), bf16[2,2048,32]{1,2,0:T(8,128)(2,1)}) %all-reduce.4.cloned.1.call-update) | async-done | bytes 262160 | tf_op jit(solution)/shard_map/psum | solution.py:81
  240.6 0.0 copy-done.3
  240.7 7.2 %broadcast_select_fusion.6 = (bf16[2,448,32]{1,2,0:T(8,128)(2,1)}, bf16[2,448,32]{1,2,0:T(8,128)(2,1)S(1)}, f32[2,448,32]{1,2,0:T(8,128)S(1)}) fusion(pred[]{:T(512)S(6)} %eq.101, f32[2,448,2048]{2,1,0:T(8,128)} %copy-done.1, bf16[2,2048,32]{1,2,0:T(8,128)(2,1)} %all-reduce.4.cloned.1.call-done, f32[2,448,32]{1,2,0:T(8,128)S(1)} %copy-done.3), kind=kOutput, calls=%fused_computation.37 | convolution fusion | flops 704786432 | bytes 7946241 | tf_op jit(solution)/shard_map/kfd,kfr->kdr/dot_general | solution.py:82
  247.9 0.8 broadcast_select_fusion.7
  248.7 66.4 %reduce-scatter.7.cloned.1.call-done = bf16[128,64]{1,0:T(8,128)(2,1)} async-done(((bf16[2048,64]{1,0:T(8,128)(2,1)}), bf16[128,64]{1,0:T(8,128)(2,1)}) %reduce-scatter.7.cloned.1.call-update) | async-done | bytes 16400
  315.1 0.8 reshape.111
  316.0 0.1 copy.64
  316.0 0.0 copy-done.4
  316.1 0.6 broadcast_select_fusion.14
  316.7 0.7 broadcast_select_fusion.15
  317.3 0.0 all-reduce.6.cloned.1.call-update
  317.4 0.0 copy-start.2
  317.4 0.0 reduce-scatter.5.cloned.1.call-start
  317.4 4.8 convolution_convert_fusion
  322.2 0.0 reduce-scatter.5.cloned.1.call-update
  322.2 0.0 copy-done.2
  322.2 4.0 convolution_convert_fusion.2
  326.2 1.2 copy.53
  327.4 0.1 copy.54
  327.5 38.8 %all_to_all.10 = bf16[2,32,8,448]{3,2,0,1:T(8,128)(2,1)S(1)} all-to-all(bf16[2,32,8,448]{3,2,0,1:T(8,128)(2,1)S(1)} %copy.54), channel_id=1, replica_groups=mesh['outer'=32,'chip'=16] {'outer'}, dimensions={1} | all-to-all | bytes 917504 | tf_op jit(solution)/shard_map/all_to_all | solution.py:55
  366.3 1.0 convolution_convert_fusion.4
  367.3 238.6 %all-reduce.6.cloned.1.call-done = (bf16[2,128,32]{1,2,0:T(8,128)(2,1)}, bf16[2,128,32]{1,2,0:T(8,128)(2,1)}, bf16[2,128,32]{1,2,0:T(8,128)(2,1)}, bf16[2,128,32...) async-done(((bf16[2,128,32]{1,2,0:T(8,128)(2,1)}, ...) | async-done | bytes 589840 | tf_op jit(solution)/shard_map/psum | solution.py:13
  605.8 1.5 select_select_fusion.1
  607.3 1.8 select_select_fusion
  609.1 64.1 %reduce-scatter.5.cloned.1.call-done = bf16[2,16,2048]{2,1,0:T(8,128)(2,1)} async-done(((bf16[2,256,2048]{2,1,0:T(8,128)(2,1)}), bf16[2,16,2048]{2,1,0:T(8,128)(2,1)}) %reduce-scatter.5.cloned.1.call-update) | async-done | bytes 131088 | tf_op jit(solution)/shard_map/reduce_scatter | solution.py:68
  (4 shorter events, 0.1 us)
Async XLA Ops:
  7.2 81.3 %copy-start = (f32[2048,32]{0,1:T(8,128)S(1)}, f32[2048,32]{0,1:T(8,128)}, u32[]{:S(2)}) copy-start(f32[2048,32]{0,1:T(8,128)} %param.16) | copy-start | bytes 786436
  7.2 21.2 %copy-start.6 = (s32[4,2]{0,1:T(2,128)S(1)}, s32[4,2]{0,1:T(2,128)}, u32[]{:S(2)}) copy-start(s32[4,2]{0,1:T(2,128)} %param.19) | copy-start | bytes 100
  7.2 78.5 %all-gather.2.cloned.1.call-start = ((), (), s32[]{:S(2)}) async-start(), calls=%async_computation.4 | async-start | bytes 2228224 | tf_op jit(solution)/shard_map/all_gather | solution.py:51
  13.8 31.5 %all-to-all-start.1 = ((bf16[2,32,8,448]{3,2,0,1:T(8,128)(2,1)}), bf16[2,32,8,448]{3,2,0,1:T(8,128)(2,1)S(1)}, u32[]{:S(2)}, u32[]{:S(2)}) async-start(bf16[2,32,8,448]{3,2,0,1:T(8,128)(2,1)} %copy.57), calls=%async_computation.1 | async-start | bytes 1048576 | tf_op jit(solution)/shard_map/all_to_all | solution.py:48
  28.3 212.4 %all-reduce.4.cloned.1.call-start = ((), (), s32[]{:S(2)}) async-start(), calls=%async_computation.6 | async-start | bytes 524288 | tf_op jit(solution)/shard_map/psum | solution.py:81
  88.4 6.5 copy-start.1
  88.4 6.5 copy-start.5
  100.1 140.5 %copy-start.3 = (f32[2,448,32]{1,2,0:T(8,128)S(1)}, f32[2,448,32]{1,2,0:T(8,128)}, u32[]{:S(2)}) copy-start(f32[2,448,32]{1,2,0:T(8,128)} %param.18) | copy-start | bytes 344068
  100.1 215.0 %reduce-scatter.7.cloned.1.call-start = ((), (), s32[]{:S(2)}) async-start(), calls=%async_computation.7 | async-start | bytes 557056
  109.8 206.2 %copy-start.4 = (f32[2,128,32]{1,2,0:T(8,128)S(1)}, f32[2,128,32]{1,2,0:T(8,128)}, u32[]{:S(2)}) copy-start(f32[2,128,32]{1,2,0:T(8,128)} %param.17) | copy-start | bytes 98308
  109.8 496.0 %all-reduce.6.cloned.1.call-start = ((), (), s32[]{:S(2)}) async-start(), calls=%async_computation.8 | async-start | bytes 1310720 | tf_op jit(solution)/shard_map/psum | solution.py:13
  317.4 4.8 copy-start.2
  317.4 355.8 %reduce-scatter.5.cloned.1.call-start = ((), (), s32[]{:S(2)}) async-start(), calls=%async_computation.5 | async-start | bytes 2228224 | tf_op jit(solution)/shard_map/reduce_scatter | solution.py:68
Sparse Core Ops, SparseCore 0:
  10.1 75.5 all-gather.1
  100.3 140.3 all-reduce.3
  243.7 71.3 reduce-scatter.6
  319.6 286.1 all-reduce.5
  609.3 63.8 reduce-scatter.4
where the time goes:
time: 690 us; the launch traced here: 680 us
  waiting for transfers between devices  552 us (80%)
  matrix products  40.1 us (6%)
  blocking collectives  38.8 us (6%)
  between operations  19.1 us (3%)
  starting transfers between devices  14.8 us (2%)
  local copies, waits for them, and re-layouts  8.07 us (1%)
    psum x1, waiting for transfers between devices, broadcast(): return lax.psum(jnp.where(mine, shard, jnp.zeros_like(shard)), axis)  239 us
    psum x1, waiting for transfers between devices, on_device(): lax.psum(cols_part.astype(jnp.bfloat16), 'chip').astype(jnp.float32)  131 us
    unnamed x6, waiting for transfers between devices  67.2 us
    reduce_scatter x1, waiting for transfers between devices, on_device(): lax.psum_scatter(partial_value.astype(jnp.bfloat16), 'chip', scatter_dime...  64.1 us
    all_gather x1, waiting for transfers between devices, on_device(): full_rows = lax.all_gather(hidden, 'chip', axis=1, tiled=True)  40.4 us
    all_to_all x1, blocking collectives, on_device(): lax.all_to_all(expert_out.reshape(local_experts, outer_size, slot_count,...  38.8 us
    all_to_all x1, starting transfers between devices, on_device(): lax.all_to_all(outgoing, 'outer', split_axis=1, concat_axis=1, tiled=True)  14.4 us
  transfers between devices with their start and end apart: 6, of which 6 were waited for; matrix products, arithmetic and copies ran while one was open for 6% of the time, Pallas kernels for 0%

commit v1 on v0

--- a/solution.py
+++ b/solution.py
@@ -74,43 +74,38 @@
     scale_left = 10.0 / (
         expert_rows * (model_width / math.sqrt(hidden_width) + math.sqrt(model_width))
     )
-    weight_grad = jnp.einsum(
-        "kmf,kmd->kfd", full_rows, expert_grad, preferred_element_type=jnp.float32
-    )
-    cols_part = jnp.einsum("kfd,dr->kfr", weight_grad, omega, precision=highest)
-    sketch_cols = lax.psum(cols_part.astype(jnp.bfloat16), "chip").astype(jnp.float32)
-    right_step = jnp.einsum("kfd,kfr->kdr", weight_grad, sketch_cols, precision=highest)
-    width_side = jnp.einsum("kfd,fr->kdr", weight_grad, psi, precision=highest)
-    rows_part = jnp.einsum("kfd,kdr->kfr", weight_grad, width_side, precision=highest)
-    left_step = lax.psum_scatter(
-        rows_part.astype(jnp.bfloat16), "chip", scatter_dimension=1, tiled=True
-    ).astype(jnp.float32)
+    wide_rows = full_rows.astype(jnp.float32)
+    wide_grad = expert_grad.astype(jnp.float32)
+    row_cols = lax.psum(jnp.einsum("kmd,dr->kmr", wide_grad, omega, precision=highest), "chip")
+    sketch_cols = jnp.einsum("kmf,kmr->kfr", wide_rows, row_cols, precision=highest)
+    row_width = jnp.einsum("kmf,kfr->kmr", wide_rows, sketch_cols, precision=highest)
+    right_step = jnp.einsum("kmd,kmr->kdr", wide_grad, row_width, precision=highest)
+    row_psi = jnp.einsum("kmf,fr->kmr", wide_rows, psi, precision=highest)
+    width_side = jnp.einsum("kmd,kmr->kdr", wide_grad, row_psi, precision=highest)
+    row_left = lax.psum(jnp.einsum("kmd,kdr->kmr", wide_grad, width_side, precision=highest), "chip")
+    own = hidden_width // chip_size
+    own_rows = lax.dynamic_slice_in_dim(wide_rows, lax.axis_index("chip") * own, own, 2)
+    left_step = jnp.einsum("kmf,kmr->kfr", own_rows, row_left, precision=highest)
     right_new = 0.5 * right_old + 0.5 * scale_right * right_step
     left_new = 0.5 * left_old + 0.5 * scale_left * left_step
     outer_index = lax.axis_index("outer")
-
-    def fetch(payload, root_group):
-        return (
-            broadcast(payload[0].astype(jnp.bfloat16), "outer", root_group).astype(jnp.float32),
-            broadcast(payload[1].astype(jnp.bfloat16), "outer", root_group).astype(jnp.float32),
-        )
-
-    left_moved, right_moved = (left_new, right_new)
+    source = outer_index
     for move_index in range(moves.shape[0]):
         from_group = moves[move_index, 0]
         to_group = moves[move_index, 1]
-        from_left, from_right = fetch((left_new, right_new), from_group)
-        to_left, to_right = fetch((left_new, right_new), to_group)
-        left_moved = jnp.where(
-            outer_index == to_group,
-            from_left,
-            jnp.where(outer_index == from_group, to_left, left_moved),
+        source = jnp.where(
+            outer_index == from_group,
+            to_group,
+            jnp.where(outer_index == to_group, from_group, source),
         )
-        right_moved = jnp.where(
-            outer_index == to_group,
-            from_right,
-            jnp.where(outer_index == from_group, to_right, right_moved),
-        )
+    payload = jnp.concatenate([left_new, right_new], axis=1).astype(jnp.bfloat16)
+    payload = payload.reshape(-1, 128)
+    gathered = lax.all_gather(payload, "outer", axis=0, tiled=False)
+    arrived = lax.dynamic_index_in_dim(gathered, source, 0, keepdims=False)
+    arrived = arrived.reshape(local_experts, own + column_count, -1).astype(jnp.float32)
+    stays = source == outer_index
+    left_moved = jnp.where(stays, left_new, arrived[:, :own])
+    right_moved = jnp.where(stays, right_new, arrived[:, own:])
     return (mixed, hidden_grad, left_moved, right_moved)
 
 

time: 690 us -> 417 us (0.60)
  the two profiles are of different devices: /device:TPU:1 before, /device:TPU:4 now
where the time goes in v1:
time: 417 us
  waiting for transfers between devices  321 us (77%)
  blocking collectives  30.9 us (7%)
  between operations  24.2 us (6%)
  matrix products  21 us (5%)
  starting transfers between devices  10.7 us (3%)
  local copies, waits for them, and re-layouts  5.59 us (1%)
    psum x1, waiting for transfers between devices, on_device(): lax.psum(jnp.einsum('kmd,kdr->kmr', wide_grad, width_side, precision=high...  141 us
    reduce_scatter x1, waiting for transfers between devices, on_device(): lax.psum_scatter(partial_value.astype(jnp.bfloat16), 'chip', scatter_dime...  76.6 us
    all_gather x1, waiting for transfers between devices, on_device(): full_rows = lax.all_gather(hidden, 'chip', axis=1, tiled=True)  47.4 us
    all_gather x1, waiting for transfers between devices, on_device(): gathered = lax.all_gather(payload, 'outer', axis=0, tiled=False)  47.1 us
    all_to_all x1, blocking collectives, on_device(): lax.all_to_all(outgoing, 'outer', split_axis=1, concat_axis=1, tiled=True)  30.9 us
    all_to_all x1, starting transfers between devices, on_device(): lax.all_to_all(expert_out.reshape(local_experts, outer_size, slot_count,...  10.5 us
  transfers between devices with their start and end apart: 5, of which 5 were waited for; matrix products, arithmetic and copies ran while one was open for 5% of the time, Pallas kernels for 0%

profile of v1, /device:TPU:4, one launch (start us, length us, event | category | flops | bytes accessed | tf_op | source)
XLA Modules:
  0.0 416.7 jit_solution(16376493568448336488)
XLA Ops:
  7.2 0.0 copy-start
  7.2 0.0 all-gather.3.cloned.1.call-start
  7.2 0.7 all-gather.3.cloned.1.call-update
  7.9 0.0 all-reduce.3.cloned.1.call-start
  8.0 0.8 copy.54
  8.7 0.1 eq.72
  8.8 0.1 eq.68
  8.9 0.8 copy.61
  9.7 0.9 reduce-window.6
  10.6 0.0 copy-start.3
  10.6 0.2 slice_reduce_fusion
  10.9 0.1 fusion.20
  11.0 0.1 reduce_sum.21
  11.1 0.3 select_reduce_fusion
  11.4 1.4 convolution_convert_fusion.2
  12.8 0.2 copy.65
  13.0 0.1 copy.66
  13.1 30.9 %all_to_all.10 = bf16[2,32,8,448]{3,2,0,1:T(8,128)(2,1)S(1)} all-to-all(bf16[2,32,8,448]{3,2,0,1:T(8,128)(2,1)S(1)} %copy.66), channel_id=1, replica_groups=mesh['outer'=32,'chip'=16] {'outer'}, dimensions={1} | all-to-all | bytes 917504 | tf_op jit(solution)/shard_map/all_to_all | solution.py:48
  44.0 0.0 copy-done.3
  44.0 1.2 fusion.3
  45.2 47.4 %all-gather.3.cloned.1.call-done = bf16[2,256,2048]{2,1,0:T(8,128)(2,1)} async-done(((bf16[2,16,2048]{2,1,0:T(8,128)(2,1)}), bf16[2,256,2048]{2,1,0:T(8,128)(2,1)}) %all-gather.3.cloned.1.call-update) | async-done | bytes 2097168 | tf_op jit(solution)/shard_map/all_gather | solution.py:51
  92.7 0.0 copy-done
  92.7 0.0 copy-start.1
  92.7 3.6 fusion.15
  96.3 0.3 fusion.7
  96.7 1.2 fusion.5
  97.9 0.0 all-reduce.3.cloned.1.call-update
  97.9 0.0 all-gather.5.cloned.1.call-start
  98.0 140.6 %all-reduce.3.cloned.1.call-done = (f32[2,256,32]{1,2,0:T(8,128)}, f32[2,256,32]{1,2,0:T(8,128)}) async-done(((f32[2,256,32]{1,2,0:T(8,128)}, f32[2,256,32]{1,2,0:T(8,128)}), (f32[2,256,32]{1,2,0:T(8,128)}, f32[2,256,32]{1,2,0:T(8,128)})) %all-reduce.3.cloned.1.call-update) | async-done | bytes 131088 | tf_op jit(solution)/shard_map/psum | solution.py:85
  238.6 0.0 copy-done.1
  238.6 0.0 copy-start.2
  238.6 2.0 fusion.36
  240.6 0.0 copy-start.4
  240.6 0.0 copy-start.5
  240.6 1.9 fusion.37
  242.5 0.0 copy-done.2
  242.5 0.4 fusion.34
  242.9 0.0 copy-done.4
  242.9 0.0 copy-done.5
  242.9 0.2 fusion.35
  243.1 0.2 copy.73
  243.3 0.8 convert_element_type.47
  244.2 0.0 all-gather.5.cloned.1.call-update
  244.2 0.0 reduce-scatter.2.cloned.1.call-start
  244.2 4.6 %convolution_convert_fusion = bf16[2,256,2048]{2,1,0:T(8,128)(2,1)} fusion(bf16[2,2048,448]{1,2,0:T(8,128)(2,1)} %param.11, bf16[2,32,8,448]{3,2,0,1:T(8,128)(2,1)S(1)} %all_to_all.10), kind=kOutput, calls=%fused_computation | convolution fusion | flops 940572672 | bytes 6225920 | tf_op jit(solution)/shard_map/kmd,kfd->kmf/dot_general | solution.py:65
  248.8 0.0 reduce-scatter.2.cloned.1.call-update
  248.9 3.2 convolution_convert_fusion.1
  252.1 0.0 copy-start.6
  252.1 0.2 copy.62
  252.3 0.9 copy.63
  253.1 10.5 %all-to-all-start = ((bf16[2,32,8,448]{3,2,0,1:T(8,128)(2,1)}), bf16[2,32,8,448]{3,2,0,1:T(8,128)(2,1)S(1)}, u32[]{:S(2)}, u32[]{:S(2)}) async-start(bf16[2,32,8,448]{3,2,0,1:T(8,128)(2,1)} %copy.63), calls=%async_computation | async-start | bytes 1048576 | tf_op jit(solution)/shard_map/all_to_all | solution.py:55
  263.7 0.0 copy-done.6
  263.7 0.7 fusion.33
  274.6 8.2 %all-to-all-done = bf16[2,32,8,448]{3,2,0,1:T(8,128)(2,1)S(1)} async-done(((bf16[2,32,8,448]{3,2,0,1:T(8,128)(2,1)}), bf16[2,32,8,448]{3,2,0,1:T(8,128)(2,1)S(1)}, u32[]{:S(2)}, u32[]{:S(2)}) %all-to-all-start) | async-done | bytes 458784 | tf_op jit(solution)/shard_map/all_to_all | solution.py:55
  282.8 1.0 convolution_convert_fusion.3
  283.8 47.1 %all-gather.5.cloned.1.call-done = bf16[32,288,128]{2,1,0:T(8,128)(2,1)} async-done(((bf16[1,288,128]{2,1,0:T(8,128)(2,1)}), bf16[32,288,128]{2,1,0:T(8,128)(2,1)}) %all-gather.5.cloned.1.call-update) | async-done | bytes 2359312 | tf_op jit(solution)/shard_map/all_gather | solution.py:103
  330.9 0.9 dynamic-slice_convert_fusion
  331.8 0.2 reshape.123
  332.0 0.2 copy.82
  332.2 0.1 copy.81
  332.3 0.6 broadcast_select_fusion.1
  332.9 0.7 broadcast_select_fusion
  333.6 76.6 %reduce-scatter.2.cloned.1.call-done = bf16[2,16,2048]{2,1,0:T(8,128)(2,1)} async-done(((bf16[2,256,2048]{2,1,0:T(8,128)(2,1)}), bf16[2,16,2048]{2,1,0:T(8,128)(2,1)}) %reduce-scatter.2.cloned.1.call-update) | async-done | bytes 131088 | tf_op jit(solution)/shard_map/reduce_scatter | solution.py:68
  (7 shorter events, 0.2 us)
Async XLA Ops:
  7.2 85.5 %copy-start = (f32[2048,32]{0,1:T(8,128)S(1)}, f32[2048,32]{0,1:T(8,128)}, u32[]{:S(2)}) copy-start(f32[2048,32]{0,1:T(8,128)} %param.16) | copy-start | bytes 786436
  7.2 85.5 %all-gather.3.cloned.1.call-start = ((), (), s32[]{:S(2)}) async-start(), calls=%async_computation.3 | async-start | bytes 2228224 | tf_op jit(solution)/shard_map/all_gather | solution.py:51
  7.9 230.6 %all-reduce.3.cloned.1.call-start = ((), (), s32[]{:S(2)}) async-start(), calls=%async_computation.6 | async-start | bytes 262144 | tf_op jit(solution)/shard_map/psum | solution.py:85
  10.6 33.4 %copy-start.3 = (f32[448,32]{0,1:T(8,128)S(1)}, f32[448,32]{0,1:T(8,128)}, u32[]{:S(2)}) copy-start(f32[448,32]{0,1:T(8,128)} %param.15) | copy-start | bytes 172036
  92.7 145.9 %copy-start.1 = (bf16[2,256,2048]{2,1,0:T(8,128)(2,1)S(1)}, bf16[2,256,2048]{2,1,0:T(8,128)(2,1)}, u32[]{:S(2)}) copy-start(bf16[2,256,2048]{2,1,0:T(8,128)(2,1)} %all-gather.3.cloned.1.call-done) | copy-start | bytes 6291460
  97.9 233.0 %all-gather.5.cloned.1.call-start = ((), (), s32[]{:S(2)}) async-start(), calls=%async_computation.5 | async-start | bytes 2433024 | tf_op jit(solution)/shard_map/all_gather | solution.py:103
  238.6 4.0 copy-start.2
  240.6 2.3 copy-start.4
  240.6 2.3 copy-start.5
  244.2 166.0 %reduce-scatter.2.cloned.1.call-start = ((), (), s32[]{:S(2)}) async-start(), calls=%async_computation.4 | async-start | bytes 2228224 | tf_op jit(solution)/shard_map/reduce_scatter | solution.py:68
  252.1 11.6 %copy-start.6 = (s32[4,2]{0,1:T(2,128)S(1)}, s32[4,2]{0,1:T(2,128)}, u32[]{:S(2)}) copy-start(s32[4,2]{0,1:T(2,128)} %param.19) | copy-start | bytes 100
  253.1 29.6 %all-to-all-start = ((bf16[2,32,8,448]{3,2,0,1:T(8,128)(2,1)}), bf16[2,32,8,448]{3,2,0,1:T(8,128)(2,1)S(1)}, u32[]{:S(2)}, u32[]{:S(2)}) async-start(bf16[2,32,8,448]{3,2,0,1:T(8,128)(2,1)} %copy.63), calls=%async_computation | async-start | bytes 1048576 | tf_op jit(solution)/shard_map/all_to_all | solution.py:55
Sparse Core Ops, SparseCore 0:
  10.1 82.5 all-gather.2
  98.0 140.4 all-reduce.2
  244.3 86.5 all-gather.4
  334.4 75.7 reduce-scatter.1

commit v2 on v1

v2 whole, which is shorter than its diff:
```python
import functools
import math

import jax
import jax.numpy as jnp
from jax import lax
from jax.experimental import pallas as pl
from jax.experimental.pallas import tpu as pltpu
from jax.sharding import PartitionSpec as P

MESH = pl.DeviceIdType.MESH
WAY = (1, -1)


def dot(a, b, a_dim, b_dim):
    return lax.dot_general(
        a, b, (((a_dim,), (b_dim,)), ((), ())), preferred_element_type=jnp.float32
    )


def halves(a):
    high = a.astype(jnp.bfloat16)
    return high, (a - high.astype(jnp.float32)).astype(jnp.bfloat16)


def dot_halves(a, b, b_dim):
    high, low = halves(a)
    both = dot(jnp.concatenate([high, low], axis=0), b, 1, b_dim)
    return both[: a.shape[0]] + both[a.shape[0] :]


def kernel(
    sizes,
    hid, wt, og, routes, gates, om, ps, left_old, right_old, moves,
    mixed, hidden_grad, left_out, right_out,
    full, wv, assign, ob, gb, grad, part, rs_in, x_in, eo, rb,
    us, ui, uo, ua, vs, vi, vo, va, rn, ln, pay, tz, sel, t2,
    w_sem, ag_s, ag_r, agx_s, agx_r, rs_s, rs_r, rsx_s, rsx_r, one_s, one_r,
):
    outer_size, chip_size, zn, yn, scale_left, scale_right = sizes
    o, c = lax.axis_index("outer"), lax.axis_index("chip")
    z, sub = o // 4, o % 4
    y, xl = c // 2, c % 2
    experts, block, hidden_width = hid.shape
    columns = og.shape[1]
    rank = om.shape[0]
    rows_all = full.shape[1]
    own = left_old.shape[2]
    steps = yn - 1

    barrier = pltpu.get_barrier_semaphore()

    @pl.loop(1, outer_size)
    def _(i):
        pl.semaphore_signal(barrier, inc=1, device_id=((o + i) % outer_size, c), device_id_type=MESH)

    @pl.loop(1, chip_size)
    def _(i):
        pl.semaphore_signal(barrier, inc=1, device_id=(o, (c + i) % chip_size), device_id_type=MESH)

    w_copy = pltpu.make_async_copy(wt, wv, w_sem)
    w_copy.start()

    routes_now, gates_now = routes[...], gates[...]
    tokens = routes_now.shape[1]
    place = lax.broadcasted_iota(jnp.int32, assign.shape, 0)
    expert = lax.shift_right_logical(place, 3)
    slot = (place & 7).astype(jnp.float32)
    picked = jnp.zeros(assign.shape, jnp.float32)
    weight = jnp.zeros(assign.shape, jnp.float32)
    for p in range(routes_now.shape[0]):
        hit = routes_now[p : p + 1, :] == expert
        picked = picked + jnp.where(hit, 1.0, 0.0)
        weight = weight + jnp.where(hit, gates_now[p : p + 1, :], 0.0)
    earlier = lax.broadcasted_iota(jnp.int32, (tokens, tokens), 0) < lax.broadcasted_iota(
        jnp.int32, (tokens, tokens), 1
    )
    ranks = dot(picked.astype(jnp.bfloat16), jnp.where(earlier, 1.0, 0.0).astype(jnp.bfloat16), 1, 0)
    weight = jnp.where(ranks == slot, weight, 0.0)
    assign[...] = weight
    high, low = halves(weight)
    og_now = og[...]
    outgoing = dot(high, og_now, 1, 0) + dot(low, og_now, 1, 0)
    ob[...] = outgoing.astype(jnp.bfloat16).reshape(ob.shape)
    gb[o] = ob[o]

    def rows(chip):
        return pl.ds(pl.multiple_of(chip * block, block), block)

    for k in range(experts):
        full[k, rows(c), :] = hid[k]

    pl.semaphore_wait(barrier, outer_size + chip_size - 2)

    def remote(src, dst, send, recv, device):
        return pltpu.make_async_remote_copy(
            src_ref=src, dst_ref=dst, send_sem=send, recv_sem=recv, device_id=device, device_id_type=MESH
        )

    def along_y(k):
        return (o, ((y + WAY[k] + yn) % yn) * 2 + xl)

    x_partner = (o, 2 * y + 1 - xl)

    def ag_copy(k, s, j):
        source = 2 * ((y - WAY[k] * s + yn) % yn) + (xl if j == 0 else 1 - xl)
        src = hid.at[k] if s == 0 and j == 0 else full.at[k, rows(source)]
        return remote(src, full.at[k, rows(source)], ag_s.at[k, s, j], ag_r.at[k, s, j], along_y(k))

    def ag_x(k):
        return remote(hid.at[k], full.at[k, rows(c)], agx_s.at[k], agx_r.at[k], x_partner)

    def ag_step(s):
        for j in range(2):
            for k in range(experts):
                ag_copy(k, s, j).wait_recv()
                if s + 1 < steps:
                    ag_copy(k, s + 1, j).start()

    for k in range(experts):
        ag_x(k).start()
        ag_copy(k, 0, 0).start()

    def spread(src_of, dst, number, axis_size, device_of):
        @pl.loop(1, axis_size)
        def _(i):
            remote(src_of(i), dst, one_s.at[number], one_r.at[number], device_of(i)).start()

    def arrived(buf, count, number):
        ref = buf.at[pl.ds(0, count)]
        pltpu.make_async_copy(ref, ref, one_r.at[number]).wait()

    def sent(buf, count, number):
        ref = buf.at[pl.ds(0, count)]
        pltpu.make_async_copy(ref, ref, one_s.at[number]).wait()

    def other_group(i):
        return (o + i) % outer_size

    def other_chip(i):
        return (c + i) % chip_size

    spread(lambda i: ob.at[other_group(i)], gb.at[o], 0, outer_size, lambda i: (other_group(i), c))

    for k in range(experts):
        ag_x(k).wait_recv()
        ag_copy(k, 0, 1).start()

    early = min(3, steps - 1)
    for s in range(early):
        ag_step(s)

    arrived(gb, outer_size - 1, 0)
    eight = block // experts
    come = gb[...].astype(jnp.float32)
    for k in range(experts):
        grad[k] = come[:, k * eight : (k + 1) * eight, :].reshape(rows_all, columns).astype(jnp.bfloat16)

    lanes = us.shape[2]
    lane_cuts = rows_all // lanes
    piece = us.shape[1]

    def sum_send(parts, send, into, number):
        both = jnp.concatenate(parts, axis=0)
        for p in range(chip_size):
            at, cut = p // lane_cuts, p % lane_cuts
            send[p] = both[at * piece : (at + 1) * piece, cut * lanes : (cut + 1) * lanes]
        into[c] = send[c]
        spread(lambda i: send.at[other_chip(i)], into.at[c], number, chip_size, lambda i: (o, other_chip(i)))

    def sum_share(into, own_sum, full_sum, number):
        arrived(into, chip_size - 1, number)
        own_sum[...] = jnp.sum(into[...], axis=0)
        full_sum[c] = own_sum[...]
        spread(lambda i: own_sum, full_sum.at[c], number + 1, chip_size, lambda i: (o, other_chip(i)))

    def sum_take(full_sum, number):
        arrived(full_sum, chip_size - 1, number + 1)
        lines = []
        for at in range(chip_size // lane_cuts):
            lines.append(
                jnp.concatenate([full_sum[at * lane_cuts + cut] for cut in range(lane_cuts)], axis=1)
            )
        both = jnp.concatenate(lines, axis=0)
        return [both[k * rank : (k + 1) * rank] for k in range(experts)]

    omega = om[...]
    sum_send([dot_halves(omega, grad[k], 1) for k in range(experts)], us, ui, 1)

    w_copy.wait()
    tile = min(512, hidden_width)

    def partial_of(k):
        @pl.loop(0, hidden_width // tile)
        def _(n):
            cut = pl.ds(pl.multiple_of(n * tile, tile), tile)
            part[k, :, cut] = dot(grad[k], wv[k, :, cut], 1, 0).astype(jnp.bfloat16)

    partial_of(0)
    ag_step(early)
    partial_of(1)
    for s in range(early + 1, steps):
        ag_step(s)

    def rs_rows(k, s, j):
        return rows(2 * ((y - WAY[k] * (s + 1) + 2 * yn) % yn) + (1 - xl if j == 0 else xl))

    def rs_copy(k, s, j):
        return remote(
            part.at[k, rs_rows(k, s, j)], rs_in.at[k, s, j], rs_s.at[k, s, j], rs_r.at[k, s, j], along_y(k)
        )

    def rs_add(k, s, j):
        rs_copy(k, s - 1, j).wait_recv()
        return part[k, rs_rows(k, s, j), :].astype(jnp.float32) + rs_in[k, s - 1, j].astype(jnp.float32)

    def rs_step(s):
        for j in range(2):
            for k in range(experts):
                part[k, rs_rows(k, s, j), :] = rs_add(k, s, j).astype(jnp.bfloat16)
                rs_copy(k, s, j).start()

    def rs_x(k):
        return remote(part.at[k, rs_rows(k, steps, 0)], x_in.at[k], rsx_s.at[k], rsx_r.at[k], x_partner)

    for j in range(2):
        for k in range(experts):
            rs_copy(k, 0, j).start()

    todo = list(range(1, steps))

    def rs_next():
        if todo:
            rs_step(todo.pop(0))

    width = ps[...]
    left_parts = []
    for k in range(experts):
        row_psi = dot_halves(width, full[k], 1)
        width_side = dot_halves(row_psi, grad[k], 0)
        left_parts.append(dot_halves(width_side, grad[k], 1))
    sum_send(left_parts, vs, vi, 3)
    sum_share(ui, uo, ua, 1)

    outputs = []
    for k in range(experts):
        outputs.append(dot(full[k], wv[k], 1, 1).reshape(outer_size, eight, columns))
        if k == 0:
            rs_next()
    eo[...] = jnp.concatenate(outputs, axis=1).astype(jnp.bfloat16)
    rb[o] = eo[o]
    spread(lambda i: eo.at[other_group(i)], rb.at[o], 5, outer_size, lambda i: (other_group(i), c))
    sum_share(vi, vo, va, 3)
    rs_next()

    row_cols = sum_take(ua, 1)
    for k in range(experts):
        sketch = dot_halves(row_cols[k], full[k], 0)
        row_width = dot_halves(sketch, full[k], 1)
        rn[k] = 0.5 * right_old[k] + 0.5 * scale_right * dot_halves(row_width, grad[k], 0)
    rs_next()
    row_left = sum_take(va, 3)
    mine = pl.ds(pl.multiple_of(c * own, own), own)
    for k in range(experts):
        ln[k] = 0.5 * left_old[k] + 0.5 * scale_left * dot_halves(row_left[k], full[k, :, mine], 0)

    for k in range(experts):
        pay[:, k * columns : (k + 1) * columns] = rn[k].astype(jnp.bfloat16)
        at = experts * columns + k * own
        pay[:, at : at + own] = ln[k].astype(jnp.bfloat16)
    tz[z] = pay[...]
    spread(lambda i: pay, tz.at[z], 6, zn, lambda i: (((z + i) % zn) * 4 + sub, c))

    def source_of(group):
        source = group
        for m in range(moves.shape[0]):
            a, b = moves[m, 0], moves[m, 1]
            source = jnp.where(group == a, b, jnp.where(group == b, a, source))
        return source

    for _ in range(2):
        rs_next()

    arrived(rb, outer_size - 1, 5)
    back = rb[...].reshape(outer_size * block, columns)
    high, low = halves(assign[...])
    mixed[...] = (dot(high, back, 0, 0) + dot(low, back, 0, 0)).astype(jnp.bfloat16)

    while todo:
        rs_next()

    arrived(tz, zn - 1, 6)
    for i in range(1, 4):
        sel[i - 1] = tz[lax.shift_right_logical(source_of(z * 4 + (sub + i) % 4), 2)]
        remote(
            sel.at[i - 1], t2.at[sub], one_s.at[7], one_r.at[7], (z * 4 + (sub + i) % 4, c)
        ).start()

    for k in range(experts):
        part[k, rs_rows(k, steps, 0), :] = rs_add(k, steps, 0).astype(jnp.bfloat16)
        rs_x(k).start()
    for k in range(experts):
        total = rs_add(k, steps, 1)
        rs_x(k).wait_recv()
        hidden_grad[k] = (total + x_in[k].astype(jnp.float32)).astype(jnp.bfloat16)

    mine_from = source_of(o)
    stays = mine_from == o
    arrived(t2, 3, 7)
    t2[sub] = tz[lax.shift_right_logical(mine_from, 2)]
    came = t2[mine_from & 3].astype(jnp.float32)
    for k in range(experts):
        right_out[k] = jnp.where(stays, rn[k], came[:, k * columns : (k + 1) * columns])
        at = experts * columns + k * own
        left_out[k] = jnp.where(stays, ln[k], came[:, at : at + own])

    for k in range(experts):
        ag_x(k).wait_send()
        rs_x(k).wait_send()
        for s in range(steps):
            for j in range(2):
                ag_copy(k, s, j).wait_send()
                rs_copy(k, s, j).wait_send()
    sent(ob, outer_size - 1, 0)
    sent(us, chip_size - 1, 1)
    sent(ua, chip_size - 1, 2)
    sent(vs, chip_size - 1, 3)
    sent(va, chip_size - 1, 4)
    sent(eo, outer_size - 1, 5)
    sent(tz, zn - 1, 6)
    sent(sel, 3, 7)


def on_device(hidden, down_weight, out_grad, routes, gates, omega, psi, left_old, right_old, moves):
    outer_size = lax.axis_size("outer")
    chip_size = lax.axis_size("chip")
    experts, hidden_width, columns = down_weight.shape
    model_width = columns * chip_size
    block = hidden.shape[1]
    rows_all = block * chip_size
    own = left_old.shape[1]
    rank = omega.shape[1]
    tokens = routes.shape[0]
    zn, yn = outer_size // 4, chip_size // 2
    scale_right = 10.0 / (rows_all * (hidden_width / math.sqrt(model_width) + math.sqrt(hidden_width)))
    scale_left = 10.0 / (rows_all * (model_width / math.sqrt(hidden_width) + math.sqrt(model_width)))
    lanes = min(rows_all, 128)
    piece = experts * rank * (rows_all // lanes) // chip_size
    pay_width = experts * (columns + own)
    bf16, f32 = jnp.bfloat16, jnp.float32
    dma = pltpu.SemaphoreType.DMA
    vmem = pl.BlockSpec(memory_space=pltpu.VMEM)
    mixed, hidden_grad, left_moved, right_moved = pl.pallas_call(
        functools.partial(kernel, (outer_size, chip_size, zn, yn, scale_left, scale_right)),
        out_shape=(
            jax.ShapeDtypeStruct(out_grad.shape, bf16),
            jax.ShapeDtypeStruct(hidden.shape, bf16),
            jax.ShapeDtypeStruct((experts, rank, own), f32),
            jax.ShapeDtypeStruct((experts, rank, columns), f32),
        ),
        in_specs=[
            vmem, pl.BlockSpec(memory_space=pl.ANY), vmem, vmem, vmem, vmem, vmem, vmem, vmem,
            pl.BlockSpec(memory_space=pltpu.SMEM),
        ],
        out_specs=(vmem,) * 4,
        scratch_shapes=[
            pltpu.VMEM((experts, rows_all, hidden_width), bf16),
            pltpu.VMEM((experts, columns, hidden_width), bf16),
            pltpu.VMEM((outer_size * block, tokens), f32),
            pltpu.VMEM((outer_size, block, columns), bf16),
            pltpu.VMEM((outer_size, block, columns), bf16),
            pltpu.VMEM((experts, rows_all, columns), bf16),
            pltpu.VMEM((experts, rows_all, hidden_width), bf16),
            pltpu.VMEM((experts, yn - 1, 2, block, hidden_width), bf16),
            pltpu.VMEM((experts, block, hidden_width), bf16),
            pltpu.VMEM((outer_size, block, columns), bf16),
            pltpu.VMEM((outer_size, block, columns), bf16),
        ]
        + [
            pltpu.VMEM((chip_size, piece, lanes), f32),
            pltpu.VMEM((chip_size, piece, lanes), f32),
            pltpu.VMEM((piece, lanes), f32),
            pltpu.VMEM((chip_size, piece, lanes), f32),
        ]
        * 2
        + [
            pltpu.VMEM((experts, rank, columns), f32),
            pltpu.VMEM((experts, rank, own), f32),
            pltpu.VMEM((rank, pay_width), bf16),
            pltpu.VMEM((zn, rank, pay_width), bf16),
            pltpu.VMEM((3, rank, pay_width), bf16),
            pltpu.VMEM((4, rank, pay_width), bf16),
            dma,
            dma((experts, yn - 1, 2)),
            dma((experts, yn - 1, 2)),
            dma((experts,)),
            dma((experts,)),
            dma((experts, yn - 1, 2)),
            dma((experts, yn - 1, 2)),
            dma((experts,)),
            dma((experts,)),
            dma((8,)),
            dma((8,)),
        ],
        compiler_params=pltpu.CompilerParams(
            collective_id=0, has_side_effects=True, vmem_limit_bytes=48 * 2**20
        ),
        name="layer",
    )(
        hidden,
        jnp.swapaxes(down_weight, 1, 2),
        out_grad,
        routes.T,
        gates.T,
        omega.T,
        psi.T,
        jnp.swapaxes(left_old, 1, 2),
        jnp.swapaxes(right_old, 1, 2),
        moves,
    )
    return (mixed, hidden_grad, jnp.swapaxes(left_moved, 1, 2), jnp.swapaxes(right_moved, 1, 2))


def solution(mesh):
    in_specs = (
        P("outer", "chip", None),
        P("outer", None, "chip"),
        P("outer", "chip"),
        P("outer", None),
        P("outer", None),
        P("chip", None),
        P(),
        P("outer", "chip", None),
        P("outer", "chip", None),
        P(),
    )
    out_specs = (
        P("outer", "chip"),
        P("outer", "chip", None),
        P("outer", "chip", None),
        P("outer", "chip", None),
    )
    return jax.shard_map(
        on_device, mesh=mesh, in_specs=in_specs, out_specs=out_specs, check_vma=False
    )
```

time: 417 us -> 101 us (0.24)
  the two profiles are of different devices: /device:TPU:4 before, /device:TPU:1 now
where the time goes in v2:
time: 101 us; the launch traced here: 100 us
  Pallas kernels  87.9 us (87%)
  local copies, waits for them, and re-layouts  11.9 us (12%)
    pallas_call x1, Pallas kernels, on_device(): pl.pallas_call(functools.partial(kernel, (outer_size, chip_size, zn, yn,...  87.9 us
    unnamed x23, local copies, waits for them, and re-layouts  11.9 us

profile of v2, /device:TPU:1, one launch (start us, length us, event | category | flops | bytes accessed | tf_op | source)
XLA Modules:
  0.0 100.4 jit_solution(15720220613995040612)
XLA Ops:
  0.6 0.8 copy.14.moves
  1.4 0.0 copy-start
  1.4 2.0 %copy-done = bf16[2,2048,448]{1,2,0:T(8,128)(2,1)S(1)} copy-done((bf16[2,2048,448]{1,2,0:T(8,128)(2,1)S(1)}, bf16[2,2048,448]{1,2,0:T(8,128)(2,1)}, u32[]{:S(2)}) %copy-start) | copy-done | bytes 3670040
  3.4 0.0 copy-start.1
  3.4 0.9 copy-done.1
  4.4 0.0 copy-start.2
  4.4 0.9 copy-done.2
  5.3 0.0 copy-start.3
  5.3 0.9 copy-done.3
  6.2 0.0 copy-start.4
  6.2 0.8 copy-done.4
  7.0 0.0 copy-start.5
  7.0 0.8 copy-done.5
  7.8 0.0 copy-start.6
  7.8 0.8 copy-done.6
  8.6 0.0 copy-start.7
  8.6 0.7 copy-done.7
  9.3 0.0 copy-start.8
  9.3 0.7 copy-done.8
  10.0 87.9 %layer.1 = (bf16[48,448]{1,0:T(8,128)(2,1)S(1)}, bf16[2,16,2048]{2,1,0:T(8,128)(2,1)S(1)}, f32[2,32,128]{2,1,0:T(8,128)S(1)}, f32[2,32,448]{2,1,0:T(8,128)S(1)}) custom-call(bf16[2,16,2048]{2,1,0:T(8,128)(2,1)S(1)} %copy-done.2, bf16[2,448,2048]{2,1,0:T(8,128)(2,1)S(1)} %bitcast.9, bf16[48,448]{1,0:T(8,128)(2,1)S(1)} %copy-done.5, s32[8,48]{1,0:T(8,128)S(1)} %bitcast.16, ...), custom_call_target="tpu_custom_call" | custom-call | tf_op jit(solution)/shard_map/layer/pallas_call | solution.py:353
  97.9 0.6 copy.19
  98.5 0.7 copy.20
  99.1 0.6 copy.21
  99.8 0.7 copy.22
Async XLA Ops:
  1.4 2.0 %copy-start = (bf16[2,2048,448]{1,2,0:T(8,128)(2,1)S(1)}, bf16[2,2048,448]{1,2,0:T(8,128)(2,1)}, u32[]{:S(2)}) copy-start(bf16[2,2048,448]{1,2,0:T(8,128)(2,1)} %param.11) | copy-start | bytes 11010052
  3.4 0.9 copy-start.1
  4.4 0.9 copy-start.2
  5.3 0.9 copy-start.3
  6.2 0.8 copy-start.4
  7.0 0.8 copy-start.5
  7.8 0.8 copy-start.6
  8.6 0.7 copy-start.7
  9.3 0.7 copy-start.8

commit v3 on v2

v3 whole, which is shorter than its diff:
```python
import functools
import math

import jax
import jax.numpy as jnp
from jax import lax
from jax.experimental import pallas as pl
from jax.experimental.pallas import tpu as pltpu
from jax.sharding import PartitionSpec as P

MESH = pl.DeviceIdType.MESH


def dot(a, b, a_dim, b_dim):
    return lax.dot_general(
        a, b, (((a_dim,), (b_dim,)), ((), ())), preferred_element_type=jnp.float32
    )


def halves(a):
    high = a.astype(jnp.bfloat16)
    return high, (a - high.astype(jnp.float32)).astype(jnp.bfloat16)


def dot_halves(a, b, b_dim):
    high, low = halves(a)
    both = dot(jnp.concatenate([high, low], axis=0), b, 1, b_dim)
    return both[: a.shape[0]] + both[a.shape[0] :]


def kernel(
    sizes,
    hid_in, wt_in, og_in, routes_in, gates_in, om_in, ps_in, left_in, right_in, moves_in,
    mixed, hidden_grad, left_out, right_out,
    hid, wv, og, routes, gates, om, ps, left_old, right_old, moves,
    full, assign, ob, gb, grad, part, rs_in, rx_in, x_in, eo, rb,
    pm, tp, uw, ur, us, ui, uo, ua, rn, ln, tzr, tzl, sel, t2,
    in_sem, tz_s, tz_r, ag_s, ag_r, agx_s, agx_r, rs_s, rs_r, rx_s, rx_r, one_s, one_r,
):
    outer_size, chip_size, zn, yn, scale_left, scale_right = sizes
    o, c = lax.axis_index("outer"), lax.axis_index("chip")
    z, sub = o // 4, o % 4
    y, xl = c // 2, c % 2
    experts, block, hidden_width = hid.shape
    columns = og.shape[1]
    rank = om.shape[0]
    rows_all = full.shape[1]
    own = left_old.shape[2]
    far = yn // 2

    barrier = pltpu.get_barrier_semaphore()

    @pl.loop(1, outer_size)
    def _(i):
        pl.semaphore_signal(barrier, inc=1, device_id=((o + i) % outer_size, c), device_id_type=MESH)

    @pl.loop(1, chip_size)
    def _(i):
        pl.semaphore_signal(barrier, inc=1, device_id=(o, (c + i) % chip_size), device_id_type=MESH)

    come_in = [
        pltpu.make_async_copy(src, dst, in_sem.at[n])
        for n, (src, dst) in enumerate(
            [
                (hid_in, hid), (routes_in, routes), (gates_in, gates), (og_in, og), (om_in, om), (ps_in, ps),
                (wt_in, wv), (left_in, left_old), (right_in, right_old), (moves_in, moves),
            ]
        )
    ]
    for copy in come_in:
        copy.start()
    def rows(chip):
        return pl.ds(pl.multiple_of(chip * block, block), block)

    come_in[0].wait()
    pl.semaphore_wait(barrier, outer_size + chip_size - 2)

    def remote(src, dst, send, recv, device):
        return pltpu.make_async_remote_copy(
            src_ref=src, dst_ref=dst, send_sem=send, recv_sem=recv, device_id=device, device_id_type=MESH
        )

    x_partner = (o, 2 * y + 1 - xl)

    def around(steps):
        return (y + steps + 2 * yn) % yn

    EXPERT = (1, 0, 0)
    FAR_WAY = (1, -1, 1)
    WAYS = (1, -1)

    def reach(d, t):
        return far if d == FAR_WAY[t] else far - 1

    def chip_of(y_at, t):
        return 2 * y_at + (1 - xl if t == 2 else xl)

    def ag_copy(d, s, t):
        source = rows(chip_of(around(-d * s), t))
        k = EXPERT[t]
        src = hid.at[k] if s == 0 and t < 2 else full.at[k, source]
        n = WAYS.index(d)
        return remote(
            src, full.at[k, source], ag_s.at[n, s, t], ag_r.at[n, s, t], (o, 2 * around(d) + xl)
        )

    def ag_x(n, k, y_at):
        source = rows(2 * y_at + xl)
        src = hid.at[k] if n < 2 else full.at[k, source]
        return remote(src, full.at[k, source], agx_s.at[n], agx_r.at[n], x_partner)

    def ag_x_of(d, s):
        return ag_x(2 + WAYS.index(d) * far + s, 1, around(-d * (s + 1)))

    def ag_step(s):
        for t in range(3):
            for d in WAYS:
                if s < reach(d, t):
                    ag_copy(d, s, t).wait_recv()
                    if s + 1 < reach(d, t):
                        ag_copy(d, s + 1, t).start()
                    if t == 0:
                        ag_x_of(d, s).start()

    ag_x(0, 0, y).start()
    for t in range(2):
        for d in WAYS:
            if reach(d, t):
                ag_copy(d, 0, t).start()
    ag_x(1, 1, y).start()

    def spread(src_of, dst, number, axis_size, device_of):
        @pl.loop(1, axis_size)
        def _(i):
            remote(src_of(i), dst, one_s.at[number], one_r.at[number], device_of(i)).start()

    def arrived(buf, count, number):
        ref = buf.at[pl.ds(0, count)]
        pltpu.make_async_copy(ref, ref, one_r.at[number]).wait()

    def sent(buf, count, number):
        ref = buf.at[pl.ds(0, count)]
        pltpu.make_async_copy(ref, ref, one_s.at[number]).wait()

    def other_group(i):
        return (o + i) % outer_size

    def other_chip(i):
        return (c + i) % chip_size

    for copy in come_in[1:5]:
        copy.wait()
    routes_now, gates_now = routes[...], gates[...]
    tokens = routes_now.shape[1]
    place = lax.broadcasted_iota(jnp.int32, assign.shape, 0)
    expert = lax.shift_right_logical(place, 3)
    slot = (place & 7).astype(jnp.float32)
    picked = jnp.zeros(assign.shape, jnp.float32)
    weight = jnp.zeros(assign.shape, jnp.float32)
    for p in range(routes_now.shape[0]):
        hit = routes_now[p : p + 1, :] == expert
        picked = picked + jnp.where(hit, 1.0, 0.0)
        weight = weight + jnp.where(hit, gates_now[p : p + 1, :], 0.0)
    earlier = lax.broadcasted_iota(jnp.int32, (tokens, tokens), 0) < lax.broadcasted_iota(
        jnp.int32, (tokens, tokens), 1
    )
    ranks = dot(picked.astype(jnp.bfloat16), jnp.where(earlier, 1.0, 0.0).astype(jnp.bfloat16), 1, 0)
    weight = jnp.where(ranks == slot, weight, 0.0)
    assign[...] = weight
    high, low = halves(weight)
    og_now = og[...]
    outgoing = dot(high, og_now, 1, 0) + dot(low, og_now, 1, 0)
    ob[...] = outgoing.astype(jnp.bfloat16).reshape(ob.shape)
    gb[o] = ob[o]

    spread(lambda i: ob.at[other_group(i)], gb.at[o], 0, outer_size, lambda i: (other_group(i), c))

    token_cols = dot_halves(om[...], og_now, 1)
    fold = rank // 2
    tp[c] = jnp.concatenate([token_cols[:fold], token_cols[fold:]], axis=1).astype(jnp.bfloat16)
    spread(lambda i: tp.at[c], tp.at[c], 2, chip_size, lambda i: (o, other_chip(i)))

    for copy in come_in[5:]:
        copy.wait()
    for k in range(experts):
        full[k, rows(c), :] = hid[k]
    psi_high, psi_low = halves(ps[...])
    pm[c] = jnp.concatenate([dot(hid[k], psi_high, 1, 1) + dot(hid[k], psi_low, 1, 1) for k in range(experts)], axis=1)
    spread(lambda i: pm.at[c], pm.at[c], 3, chip_size, lambda i: (o, other_chip(i)))

    ag_x(0, 0, y).wait_recv()
    for d in WAYS:
        if reach(d, 2):
            ag_copy(d, 0, 2).start()
    for s in range(far - 1):
        ag_step(s)

    arrived(tp, chip_size - 1, 2)
    token_cols = jnp.sum(tp[...].astype(jnp.float32), axis=0)
    token_cols = jnp.concatenate([token_cols[:, :tokens], token_cols[:, tokens:]], axis=0)
    uw[...] = dot_halves(assign[...], token_cols.astype(jnp.bfloat16), 1).astype(jnp.bfloat16).reshape(uw.shape)
    ur[o] = uw[o]
    spread(lambda i: uw.at[other_group(i)], ur.at[o], 4, outer_size, lambda i: (other_group(i), c))

    arrived(gb, outer_size - 1, 0)
    eight = block // experts
    come = gb[...].astype(jnp.float32)
    for k in range(experts):
        grad[k] = come[:, k * eight : (k + 1) * eight, :].reshape(rows_all, columns).astype(jnp.bfloat16)

    lanes = us.shape[2]
    lane_cuts = rows_all // lanes
    piece = us.shape[1]

    def sum_send(parts, send, into, number):
        both = jnp.concatenate(parts, axis=0)
        for p in range(chip_size):
            at, cut = p // lane_cuts, p % lane_cuts
            send[p] = both[at * piece : (at + 1) * piece, cut * lanes : (cut + 1) * lanes]
        into[c] = send[c]
        spread(lambda i: send.at[other_chip(i)], into.at[c], number, chip_size, lambda i: (o, other_chip(i)))

    def sum_share(into, own_sum, full_sum, number):
        arrived(into, chip_size - 1, number)
        own_sum[...] = jnp.sum(into[...], axis=0)
        full_sum[c] = own_sum[...]
        spread(lambda i: own_sum, full_sum.at[c], 8, chip_size, lambda i: (o, other_chip(i)))

    def sum_take(full_sum):
        arrived(full_sum, chip_size - 1, 8)
        lines = []
        for at in range(chip_size // lane_cuts):
            lines.append(
                jnp.concatenate([full_sum[at * lane_cuts + cut] for cut in range(lane_cuts)], axis=1)
            )
        return jnp.concatenate(lines, axis=0)

    sums = []
    arrived(pm, chip_size - 1, 3)
    row_psi = pm[...].reshape(rows_all, experts * rank)
    psi_high, psi_low = halves(row_psi)
    for k in range(experts):
        both = jnp.concatenate([psi_high[:, k * rank : (k + 1) * rank], psi_low[:, k * rank : (k + 1) * rank]], axis=1)
        both = dot(both, grad[k], 0, 0)
        sums.append(dot_halves(both[:rank] + both[rank:], grad[k], 1))
    sum_send(sums, us, ui, 1)

    tile = min(512, hidden_width)

    def partial_of(k):
        @pl.loop(0, hidden_width // tile)
        def _(n):
            cut = pl.ds(pl.multiple_of(n * tile, tile), tile)
            part[k, :, cut] = dot(grad[k], wv[k, :, cut], 1, 0).astype(jnp.bfloat16)

    def rs_rows(d, m, t):
        return rows(chip_of(around(d * m), t))

    def rs_copy(d, m, t):
        n = WAYS.index(d)
        return remote(
            part.at[EXPERT[t], rs_rows(d, m, t)],
            rs_in.at[n, m - 1, t],
            rs_s.at[n, m - 1, t],
            rs_r.at[n, m - 1, t],
            (o, 2 * around(d) + xl),
        )

    def rx_copy(r):
        src = part.at[1, rows(2 * around(r) + 1 - xl)]
        return remote(src, rx_in.at[r], rx_s.at[r], rx_r.at[r], x_partner)

    def rx_add(r):
        rx_copy(r).wait_recv()
        at = rows(2 * around(r) + xl)
        part[1, at, :] = (part[1, at, :].astype(jnp.float32) + rx_in[r].astype(jnp.float32)).astype(jnp.bfloat16)

    def rs_start(d, t):
        if t == 0:
            rx_add(d * reach(d, t) % yn)
        rs_copy(d, reach(d, t), t).start()

    def rs_first(t):
        for d in WAYS:
            if reach(d, t):
                rs_start(d, t)

    def rs_relay(d, m, t):
        if t == 0:
            rx_add(d * m % yn)
        rs_copy(d, m + 1, t).wait_recv()
        at = rs_rows(d, m, t)
        total = part[EXPERT[t], at, :].astype(jnp.float32) + rs_in[WAYS.index(d), m, t].astype(jnp.float32)
        part[EXPERT[t], at, :] = total.astype(jnp.bfloat16)
        rs_copy(d, m, t).start()

    todo = []
    for m in range(far - 1, 0, -1):
        for t in (1, 2, 0):
            if t == 0 and m == far - 1:
                todo += [functools.partial(rs_start, d, 0) for d in WAYS if reach(d, 0)]
            for d in WAYS:
                if m < reach(d, t):
                    todo.append(functools.partial(rs_relay, d, m, t))
    if far == 1:
        todo += [functools.partial(rs_start, d, 0) for d in WAYS if reach(d, 0)]

    def rs_do(count):
        for _ in range(min(count, len(todo))):
            todo.pop(0)()

    def rs_total(t):
        total = part[EXPERT[t], rs_rows(1, 0, t), :].astype(jnp.float32)
        for d in WAYS:
            if reach(d, t):
                rs_copy(d, 1, t).wait_recv()
                total = total + rs_in[WAYS.index(d), 0, t].astype(jnp.float32)
        return total

    def last_x():
        return remote(part.at[0, rs_rows(1, 0, 2)], x_in, rx_s.at[yn], rx_r.at[yn], x_partner)

    partial_of(0)
    rs_first(1)
    rs_first(2)
    ag_step(far - 1)
    partial_of(1)
    order = sorted(range(yn), key=lambda r: -min(r, yn - r))
    for r in order:
        rx_copy(r).start()
    arrived(ur, outer_size - 1, 4)
    cols = ur[...].astype(jnp.float32)
    ag_x(1, 1, y).wait_recv()
    for d in WAYS:
        for s in range(reach(d, 0)):
            ag_x_of(d, s).wait_recv()

    def tz_reach(d):
        return zn // 2 if d == -1 else zn // 2 - 1

    def tz_copy(d, s):
        at = (z - d * s + 2 * zn) % zn
        n = WAYS.index(d)
        return remote(
            tzr.at[at], tzr.at[at], tz_s.at[n, s], tz_r.at[n, s], (((z + d + zn) % zn) * 4 + sub, c)
        )

    def tz_step(s):
        for d in WAYS:
            if s < tz_reach(d):
                tz_copy(d, s).wait_recv()
                if s + 1 < tz_reach(d):
                    tz_copy(d, s + 1).start()

    for k in range(experts):
        row_cols = cols[:, k * eight : (k + 1) * eight, :].reshape(rows_all, rank).astype(jnp.bfloat16)
        sketch = dot(row_cols, full[k], 0, 0)
        row_width = dot_halves(sketch, full[k], 1)
        rn[k] = 0.5 * right_old[k] + 0.5 * scale_right * dot_halves(row_width, grad[k], 0)
        tzr[z, :, k * columns : (k + 1) * columns] = rn[k].astype(jnp.bfloat16)
    for d in WAYS:
        if tz_reach(d):
            tz_copy(d, 0).start()
    sum_share(ui, uo, ua, 1)

    outputs = []
    for k in range(experts):
        outputs.append(dot(full[k], wv[k], 1, 1).reshape(outer_size, eight, columns))
        rs_do(2)
    eo[...] = jnp.concatenate(outputs, axis=1).astype(jnp.bfloat16)
    rb[o] = eo[o]
    spread(lambda i: eo.at[other_group(i)], rb.at[o], 5, outer_size, lambda i: (other_group(i), c))
    rs_do(1)
    tz_step(0)
    rs_do(4)
    if zn > 2:
        tz_step(1)

    sums = sum_take(ua)
    mine = pl.ds(pl.multiple_of(c * own, own), own)
    for k in range(experts):
        row_left = sums[k * rank : (k + 1) * rank]
        ln[k] = 0.5 * left_old[k] + 0.5 * scale_left * dot_halves(row_left, full[k, :, mine], 0)
        tzl[z, :, k * own : (k + 1) * own] = ln[k].astype(jnp.bfloat16)
    spread(lambda i: tzl.at[z], tzl.at[z], 6, zn, lambda i: (((z + i) % zn) * 4 + sub, c))

    def source_of(group):
        source = group
        for m in range(moves.shape[1]):
            a, b = moves[0, m], moves[1, m]
            source = jnp.where(group == a, b, jnp.where(group == b, a, source))
        return source

    rs_do(2)
    rs_do(2)
    for s in range(2, zn // 2):
        tz_step(s)
        rs_do(4)

    right_width = experts * columns
    arrived(tzl, zn - 1, 6)
    for i in range(1, 4):
        at = lax.shift_right_logical(source_of(z * 4 + (sub + i) % 4), 2)
        sel[i - 1, :, :right_width] = tzr[at]
        sel[i - 1, :, right_width:] = tzl[at]
        remote(
            sel.at[i - 1], t2.at[sub], one_s.at[7], one_r.at[7], (z * 4 + (sub + i) % 4, c)
        ).start()
    mine_from = source_of(o)
    at = lax.shift_right_logical(mine_from, 2)
    t2[sub, :, :right_width] = tzr[at]
    t2[sub, :, right_width:] = tzl[at]

    rs_do(len(todo))
    part[0, rs_rows(1, 0, 2), :] = rs_total(2).astype(jnp.bfloat16)
    last_x().start()
    rx_add(0)
    hidden_grad[1] = rs_total(0).astype(jnp.bfloat16)
    total = rs_total(1)

    arrived(rb, outer_size - 1, 5)
    back = rb[...].reshape(outer_size * block, columns)
    high, low = halves(assign[...])
    mixed[...] = (dot(high, back, 0, 0) + dot(low, back, 0, 0)).astype(jnp.bfloat16)

    last_x().wait_recv()
    hidden_grad[0] = (total + x_in[...].astype(jnp.float32)).astype(jnp.bfloat16)

    stays = mine_from == o
    arrived(t2, 3, 7)
    came = t2[mine_from & 3].astype(jnp.float32)
    for k in range(experts):
        right_out[k] = jnp.where(stays, rn[k], came[:, k * columns : (k + 1) * columns])
        at = right_width + k * own
        left_out[k] = jnp.where(stays, ln[k], came[:, at : at + own])

    ag_x(0, 0, y).wait_send()
    ag_x(1, 1, y).wait_send()
    for d in WAYS:
        for s in range(reach(d, 0)):
            ag_x_of(d, s).wait_send()
        for t in range(3):
            for s in range(reach(d, t)):
                ag_copy(d, s, t).wait_send()
                rs_copy(d, s + 1, t).wait_send()
    for r in range(yn):
        rx_copy(r).wait_send()
    last_x().wait_send()
    sent(ob, outer_size - 1, 0)
    sent(us, chip_size - 1, 1)
    sent(ua, chip_size - 1, 8)
    sent(tp, chip_size - 1, 2)
    sent(pm, chip_size - 1, 3)
    sent(uw, outer_size - 1, 4)
    sent(eo, outer_size - 1, 5)
    sent(tzl, zn - 1, 6)
    sent(sel, 3, 7)
    for d in WAYS:
        for s in range(tz_reach(d)):
            tz_copy(d, s).wait_send()


def on_device(hidden, down_weight, out_grad, routes, gates, omega, psi, left_old, right_old, moves):
    outer_size = lax.axis_size("outer")
    chip_size = lax.axis_size("chip")
    experts, hidden_width, columns = down_weight.shape
    model_width = columns * chip_size
    block = hidden.shape[1]
    rows_all = block * chip_size
    own = left_old.shape[1]
    rank = omega.shape[1]
    tokens = routes.shape[0]
    zn, yn = outer_size // 4, chip_size // 2
    scale_right = 10.0 / (rows_all * (hidden_width / math.sqrt(model_width) + math.sqrt(hidden_width)))
    scale_left = 10.0 / (rows_all * (model_width / math.sqrt(hidden_width) + math.sqrt(model_width)))
    far = yn // 2
    lanes = min(rows_all, 128)
    piece = experts * rank * (rows_all // lanes) // chip_size
    pay_width = experts * (columns + own)
    bf16, f32 = jnp.bfloat16, jnp.float32
    dma = pltpu.SemaphoreType.DMA
    vmem = pl.BlockSpec(memory_space=pltpu.VMEM)
    operands = (
        hidden,
        jnp.swapaxes(down_weight, 1, 2),
        out_grad,
        routes.T,
        gates.T,
        omega.T,
        psi.T,
        jnp.swapaxes(left_old, 1, 2),
        jnp.swapaxes(right_old, 1, 2),
        moves.T,
    )
    mixed, hidden_grad, left_moved, right_moved = pl.pallas_call(
        functools.partial(kernel, (outer_size, chip_size, zn, yn, scale_left, scale_right)),
        out_shape=(
            jax.ShapeDtypeStruct(out_grad.shape, bf16),
            jax.ShapeDtypeStruct(hidden.shape, bf16),
            jax.ShapeDtypeStruct((experts, rank, own), f32),
            jax.ShapeDtypeStruct((experts, rank, columns), f32),
        ),
        in_specs=[pl.BlockSpec(memory_space=pl.ANY)] * len(operands),
        out_specs=(vmem,) * 4,
        scratch_shapes=[pltpu.VMEM(a.shape, a.dtype) for a in operands[:-1]]
        + [
            pltpu.SMEM(operands[-1].shape, jnp.int32),
            pltpu.VMEM((experts, rows_all, hidden_width), bf16),
            pltpu.VMEM((outer_size * block, tokens), f32),
            pltpu.VMEM((outer_size, block, columns), bf16),
            pltpu.VMEM((outer_size, block, columns), bf16),
            pltpu.VMEM((experts, rows_all, columns), bf16),
            pltpu.VMEM((experts, rows_all, hidden_width), bf16),
            pltpu.VMEM((2, far, 3, block, hidden_width), bf16),
            pltpu.VMEM((yn, block, hidden_width), bf16),
            pltpu.VMEM((block, hidden_width), bf16),
            pltpu.VMEM((outer_size, block, columns), bf16),
            pltpu.VMEM((outer_size, block, columns), bf16),
            pltpu.VMEM((chip_size, block, experts * rank), f32),
            pltpu.VMEM((chip_size, rank // 2, 2 * tokens), bf16),
            pltpu.VMEM((outer_size, block, rank), bf16),
            pltpu.VMEM((outer_size, block, rank), bf16),
            pltpu.VMEM((chip_size, piece, lanes), f32),
            pltpu.VMEM((chip_size, piece, lanes), f32),
            pltpu.VMEM((piece, lanes), f32),
            pltpu.VMEM((chip_size, piece, lanes), f32),
            pltpu.VMEM((experts, rank, columns), f32),
            pltpu.VMEM((experts, rank, own), f32),
            pltpu.VMEM((zn, rank, experts * columns), bf16),
            pltpu.VMEM((zn, rank, experts * own), bf16),
            pltpu.VMEM((3, rank, pay_width), bf16),
            pltpu.VMEM((4, rank, pay_width), bf16),
            dma((len(operands),)),
            dma((2, zn // 2)),
            dma((2, zn // 2)),
            dma((2, far, 3)),
            dma((2, far, 3)),
            dma((2 + 2 * far,)),
            dma((2 + 2 * far,)),
            dma((2, far, 3)),
            dma((2, far, 3)),
            dma((yn + 1,)),
            dma((yn + 1,)),
            dma((9,)),
            dma((9,)),
        ],
        compiler_params=pltpu.CompilerParams(
            collective_id=0, has_side_effects=True, vmem_limit_bytes=64 * 2**20
        ),
        name="layer",
    )(*operands)
    return (mixed, hidden_grad, jnp.swapaxes(left_moved, 1, 2), jnp.swapaxes(right_moved, 1, 2))


def solution(mesh):
    in_specs = (
        P("outer", "chip", None),
        P("outer", None, "chip"),
        P("outer", "chip"),
        P("outer", None),
        P("outer", None),
        P("chip", None),
        P(),
        P("outer", "chip", None),
        P("outer", "chip", None),
        P(),
    )
    out_specs = (
        P("outer", "chip"),
        P("outer", "chip", None),
        P("outer", "chip", None),
        P("outer", "chip", None),
    )
    return jax.shard_map(
        on_device, mesh=mesh, in_specs=in_specs, out_specs=out_specs, check_vma=False
    )
```

time: 101 us -> 84.4 us (0.84)
  Pallas kernels: 87.9 us -> 77.3 us
  local copies, waits for them, and re-layouts: 11.9 us -> 5.93 us
    pallas_call x1, Pallas kernels: 87.9 us -> 77.3 us  [on_device(): pl.pallas_call(functools.partial(kernel, (outer_size, chip_size, zn, yn,...]
    unnamed x23 -> x4, local copies, waits for them, and re-layouts: 11.9 us -> 5.93 us
where the time goes in v3:
time: 84.4 us; the launch traced here: 83.9 us
  Pallas kernels  77.3 us (92%)
  local copies, waits for them, and re-layouts  5.93 us (7%)
    pallas_call x1, Pallas kernels, on_device(): pl.pallas_call(functools.partial(kernel, (outer_size, chip_size, zn, yn,...  77.3 us
    unnamed x4, local copies, waits for them, and re-layouts  5.93 us

profile of v3, /device:TPU:1, one launch (start us, length us, event | category | flops | bytes accessed | tf_op | source)
XLA Modules:
  0.0 83.9 jit_solution(5238466206943326869)
XLA Ops:
  0.6 77.3 %layer.1 = (bf16[48,448]{1,0:T(8,128)(2,1)}, bf16[2,16,2048]{2,1,0:T(8,128)(2,1)}, f32[2,32,128]{2,1,0:T(8,128)}, f32[2,32,448]{2,1,0:T(8,128)}) custom-call(bf16[2,16,2048]{2,1,0:T(8,128)(2,1)} %hid_in.1, bf16[2,448,2048]{2,1,0:T(8,128)(2,1)} %bitcast.10, bf16[48,448]{1,0:T(8,128)(2,1)} %og_in.1, s32[8,48]{1,0:T(8,128)} %bitcast.17, f32[8,48]{1,0:T(8,128)} %bitcast.18, ...), custom_call_target="tpu_custom_call" | custom-call | tf_op jit(solution)/shard_map/layer/pallas_call | solution.py:495
  78.0 1.4 %copy.18 = bf16[48,448]{1,0:T(8,128)(2,1)} copy(bf16[48,448]{1,0:T(8,128)(2,1)} %get-tuple-element.16) | data formatting | bytes 86016
  79.4 1.6 %copy.19 = bf16[2,16,2048]{2,1,0:T(8,128)(2,1)} copy(bf16[2,16,2048]{2,1,0:T(8,128)(2,1)} %get-tuple-element.17) | data formatting | bytes 262144
  81.0 1.4 %copy.20 = f32[2,128,32]{1,2,0:T(8,128)} copy(f32[2,128,32]{1,2,0:T(8,128)} %bitcast.16) | data formatting | bytes 65536
  82.4 1.6 %copy.21 = f32[2,448,32]{1,2,0:T(8,128)} copy(f32[2,448,32]{1,2,0:T(8,128)} %bitcast.13) | data formatting | bytes 229376

commit v4 on v3

--- a/solution.py
+++ b/solution.py
@@ -31,11 +31,12 @@
 def kernel(
     sizes,
     hid_in, wt_in, og_in, routes_in, gates_in, om_in, ps_in, left_in, right_in, moves_in,
+    mixed_to, hidden_grad_to, left_to, right_to,
     mixed, hidden_grad, left_out, right_out,
     hid, wv, og, routes, gates, om, ps, left_old, right_old, moves,
     full, assign, ob, gb, grad, part, rs_in, rx_in, x_in, eo, rb,
     pm, tp, uw, ur, us, ui, uo, ua, rn, ln, tzr, tzl, sel, t2,
-    in_sem, tz_s, tz_r, ag_s, ag_r, agx_s, agx_r, rs_s, rs_r, rx_s, rx_r, one_s, one_r,
+    in_sem, out_sem, ag_s, ag_r, agx_s, agx_r, rs_s, rs_r, rx_s, rx_r, one_s, one_r,
 ):
     outer_size, chip_size, zn, yn, scale_left, scale_right = sizes
     o, c = lax.axis_index("outer"), lax.axis_index("chip")
@@ -69,6 +70,12 @@
     ]
     for copy in come_in:
         copy.start()
+    go_out = [
+        pltpu.make_async_copy(src, dst, out_sem.at[n])
+        for n, (src, dst) in enumerate(
+            [(mixed, mixed_to), (hidden_grad, hidden_grad_to), (left_out, left_to), (right_out, right_to)]
+        )
+    ]
     def rows(chip):
         return pl.ds(pl.multiple_of(chip * block, block), block)
 
@@ -328,53 +335,29 @@
     order = sorted(range(yn), key=lambda r: -min(r, yn - r))
     for r in order:
         rx_copy(r).start()
-    arrived(ur, outer_size - 1, 4)
-    cols = ur[...].astype(jnp.float32)
     ag_x(1, 1, y).wait_recv()
     for d in WAYS:
         for s in range(reach(d, 0)):
             ag_x_of(d, s).wait_recv()
 
-    def tz_reach(d):
-        return zn // 2 if d == -1 else zn // 2 - 1
-
-    def tz_copy(d, s):
-        at = (z - d * s + 2 * zn) % zn
-        n = WAYS.index(d)
-        return remote(
-            tzr.at[at], tzr.at[at], tz_s.at[n, s], tz_r.at[n, s], (((z + d + zn) % zn) * 4 + sub, c)
-        )
-
-    def tz_step(s):
-        for d in WAYS:
-            if s < tz_reach(d):
-                tz_copy(d, s).wait_recv()
-                if s + 1 < tz_reach(d):
-                    tz_copy(d, s + 1).start()
-
+    outputs = []
+    for k in range(experts):
+        outputs.append(dot(full[k], wv[k], 1, 1).reshape(outer_size, eight, columns))
+    eo[...] = jnp.concatenate(outputs, axis=1).astype(jnp.bfloat16)
+    rb[o] = eo[o]
+    spread(lambda i: eo.at[other_group(i)], rb.at[o], 5, outer_size, lambda i: (other_group(i), c))
+    rs_do(5)
+    arrived(ur, outer_size - 1, 4)
+    cols = ur[...].astype(jnp.float32)
     for k in range(experts):
         row_cols = cols[:, k * eight : (k + 1) * eight, :].reshape(rows_all, rank).astype(jnp.bfloat16)
         sketch = dot(row_cols, full[k], 0, 0)
         row_width = dot_halves(sketch, full[k], 1)
         rn[k] = 0.5 * right_old[k] + 0.5 * scale_right * dot_halves(row_width, grad[k], 0)
         tzr[z, :, k * columns : (k + 1) * columns] = rn[k].astype(jnp.bfloat16)
-    for d in WAYS:
-        if tz_reach(d):
-            tz_copy(d, 0).start()
+    spread(lambda i: tzr.at[z], tzr.at[z], 9, zn, lambda i: (((z + i) % zn) * 4 + sub, c))
     sum_share(ui, uo, ua, 1)
-
-    outputs = []
-    for k in range(experts):
-        outputs.append(dot(full[k], wv[k], 1, 1).reshape(outer_size, eight, columns))
-        rs_do(2)
-    eo[...] = jnp.concatenate(outputs, axis=1).astype(jnp.bfloat16)
-    rb[o] = eo[o]
-    spread(lambda i: eo.at[other_group(i)], rb.at[o], 5, outer_size, lambda i: (other_group(i), c))
-    rs_do(1)
-    tz_step(0)
-    rs_do(4)
-    if zn > 2:
-        tz_step(1)
+    rs_do(6)
 
     sums = sum_take(ua)
     mine = pl.ds(pl.multiple_of(c * own, own), own)
@@ -391,11 +374,10 @@
             source = jnp.where(group == a, b, jnp.where(group == b, a, source))
         return source
 
-    rs_do(2)
-    rs_do(2)
-    for s in range(2, zn // 2):
-        tz_step(s)
-        rs_do(4)
+    rs_do(6)
+    part[0, rs_rows(1, 0, 2), :] = rs_total(2).astype(jnp.bfloat16)
+    last_x().start()
+    arrived(tzr, zn - 1, 9)
 
     right_width = experts * columns
     arrived(tzl, zn - 1, 6)
@@ -411,9 +393,6 @@
     t2[sub, :, :right_width] = tzr[at]
     t2[sub, :, right_width:] = tzl[at]
 
-    rs_do(len(todo))
-    part[0, rs_rows(1, 0, 2), :] = rs_total(2).astype(jnp.bfloat16)
-    last_x().start()
     rx_add(0)
     hidden_grad[1] = rs_total(0).astype(jnp.bfloat16)
     total = rs_total(1)
@@ -423,9 +402,11 @@
     high, low = halves(assign[...])
     mixed[...] = (dot(high, back, 0, 0) + dot(low, back, 0, 0)).astype(jnp.bfloat16)
 
+    go_out[0].start()
     last_x().wait_recv()
     hidden_grad[0] = (total + x_in[...].astype(jnp.float32)).astype(jnp.bfloat16)
 
+    go_out[1].start()
     stays = mine_from == o
     arrived(t2, 3, 7)
     came = t2[mine_from & 3].astype(jnp.float32)
@@ -433,6 +414,9 @@
         right_out[k] = jnp.where(stays, rn[k], came[:, k * columns : (k + 1) * columns])
         at = right_width + k * own
         left_out[k] = jnp.where(stays, ln[k], came[:, at : at + own])
+
+    go_out[2].start()
+    go_out[3].start()
 
     ag_x(0, 0, y).wait_send()
     ag_x(1, 1, y).wait_send()
@@ -455,9 +439,23 @@
     sent(eo, outer_size - 1, 5)
     sent(tzl, zn - 1, 6)
     sent(sel, 3, 7)
-    for d in WAYS:
-        for s in range(tz_reach(d)):
-            tz_copy(d, s).wait_send()
+    sent(tzr, zn - 1, 9)
+    for copy in go_out:
+        copy.wait()
+
+
+def hand_over(*refs):
+    count = (len(refs) - 2) // 3
+    into, out, held = refs[:count], refs[count : 2 * count], refs[2 * count : 3 * count]
+    come = [pltpu.make_async_copy(into[n], held[n], refs[-2].at[n]) for n in range(count)]
+    leave = [pltpu.make_async_copy(held[n], out[n], refs[-1].at[n]) for n in range(count)]
+    for copy in come:
+        copy.start()
+    for n in range(count):
+        come[n].wait()
+        leave[n].start()
+    for copy in leave:
+        copy.wait()
 
 
 def on_device(hidden, down_weight, out_grad, routes, gates, omega, psi, left_old, right_old, moves):
@@ -479,7 +477,6 @@
     pay_width = experts * (columns + own)
     bf16, f32 = jnp.bfloat16, jnp.float32
     dma = pltpu.SemaphoreType.DMA
-    vmem = pl.BlockSpec(memory_space=pltpu.VMEM)
     operands = (
         hidden,
         jnp.swapaxes(down_weight, 1, 2),
@@ -492,17 +489,18 @@
         jnp.swapaxes(right_old, 1, 2),
         moves.T,
     )
-    mixed, hidden_grad, left_moved, right_moved = pl.pallas_call(
+    results = (
+        jax.ShapeDtypeStruct(out_grad.shape, bf16),
+        jax.ShapeDtypeStruct(hidden.shape, bf16),
+        jax.ShapeDtypeStruct((experts, rank, own), f32),
+        jax.ShapeDtypeStruct((experts, rank, columns), f32),
+    )
+    done = pl.pallas_call(
         functools.partial(kernel, (outer_size, chip_size, zn, yn, scale_left, scale_right)),
-        out_shape=(
-            jax.ShapeDtypeStruct(out_grad.shape, bf16),
-            jax.ShapeDtypeStruct(hidden.shape, bf16),
-            jax.ShapeDtypeStruct((experts, rank, own), f32),
-            jax.ShapeDtypeStruct((experts, rank, columns), f32),
-        ),
+        out_shape=results,
         in_specs=[pl.BlockSpec(memory_space=pl.ANY)] * len(operands),
-        out_specs=(vmem,) * 4,
-        scratch_shapes=[pltpu.VMEM(a.shape, a.dtype) for a in operands[:-1]]
+        out_specs=(pl.BlockSpec(memory_space=pl.ANY),) * 4,
+        scratch_shapes=[pltpu.VMEM(a.shape, a.dtype) for a in results + operands[:-1]]
         + [
             pltpu.SMEM(operands[-1].shape, jnp.int32),
             pltpu.VMEM((experts, rows_all, hidden_width), bf16),
@@ -531,8 +529,7 @@
             pltpu.VMEM((3, rank, pay_width), bf16),
             pltpu.VMEM((4, rank, pay_width), bf16),
             dma((len(operands),)),
-            dma((2, zn // 2)),
-            dma((2, zn // 2)),
+            dma((len(results),)),
             dma((2, far, 3)),
             dma((2, far, 3)),
             dma((2 + 2 * far,)),
@@ -541,14 +538,22 @@
             dma((2, far, 3)),
             dma((yn + 1,)),
             dma((yn + 1,)),
-            dma((9,)),
-            dma((9,)),
+            dma((10,)),
+            dma((10,)),
         ],
         compiler_params=pltpu.CompilerParams(
             collective_id=0, has_side_effects=True, vmem_limit_bytes=64 * 2**20
         ),
         name="layer",
     )(*operands)
+    mixed, hidden_grad, left_moved, right_moved = pl.pallas_call(
+        hand_over,
+        out_shape=results,
+        in_specs=[pl.BlockSpec(memory_space=pl.ANY)] * len(results),
+        out_specs=(pl.BlockSpec(memory_space=pl.ANY),) * len(results),
+        scratch_shapes=[pltpu.VMEM(a.shape, a.dtype) for a in results] + [dma((len(results),))] * 2,
+        name="hand_over",
+    )(*done)
     return (mixed, hidden_grad, jnp.swapaxes(left_moved, 1, 2), jnp.swapaxes(right_moved, 1, 2))
 
 

time: 84.4 us -> 78.5 us (0.930)
  local copies, waits for them, and re-layouts: 5.93 us -> 0 us
    unnamed x4 -> x0, local copies, waits for them, and re-layouts: 5.93 us -> none
    pallas_call x0 -> x1, Pallas kernels: none -> 1.74 us  [on_device(): pl.pallas_call(hand_over, out_shape=results, in_specs=[pl.BlockSpec(memor...]
    pallas_call x1, Pallas kernels: 77.3 us -> 75.9 us  [on_device(): pl.pallas_call(functools.partial(kernel, (outer_size, chip_size, zn, yn,...]
where the time goes in v4:
time: 78.5 us; the launch traced here: 78.3 us
  Pallas kernels  77.7 us (99%)
    pallas_call x1, Pallas kernels, on_device(): pl.pallas_call(functools.partial(kernel, (outer_size, chip_size, zn, yn,...  75.9 us
    pallas_call x1, Pallas kernels, on_device(): pl.pallas_call(hand_over, out_shape=results, in_specs=[pl.BlockSpec(memor...  1.74 us

profile of v4, /device:TPU:1, one launch (start us, length us, event | category | flops | bytes accessed | tf_op | source)
XLA Modules:
  0.0 78.3 jit_solution(6310183062859671587)
XLA Ops:
  0.6 75.9 %layer.1 = (bf16[48,448]{1,0:T(8,128)(2,1)}, bf16[2,16,2048]{2,1,0:T(8,128)(2,1)}, f32[2,32,128]{2,1,0:T(8,128)}, f32[2,32,448]{2,1,0:T(8,128)}) custom-call(bf16[2,16,2048]{2,1,0:T(8,128)(2,1)} %hid_in.1, bf16[2,448,2048]{2,1,0:T(8,128)(2,1)} %bitcast.10, bf16[48,448]{1,0:T(8,128)(2,1)} %og_in.1, s32[8,48]{1,0:T(8,128)} %bitcast.15, f32[8,48]{1,0:T(8,128)} %bitcast.16, ...), custom_call_target="tpu_custom_call" | custom-call | tf_op jit(solution)/shard_map/layer/pallas_call | solution.py:498
  76.6 1.7 %hand_over.1 = (bf16[48,448]{1,0:T(8,128)(2,1)}, bf16[2,16,2048]{2,1,0:T(8,128)(2,1)}, f32[2,32,128]{2,1,0:T(8,128)}, f32[2,32,448]{2,1,0:T(8,128)}) custom-call(bf16[48,448]{1,0:T(8,128)(2,1)} %get-tuple-element.12.refs_0_, bf16[2,16,2048]{2,1,0:T(8,128)(2,1)} %get-tuple-element.13.refs_1_, f32[2,32,128]{2,1,0:T(8,128)} %get-tuple-element.14.refs_2_, ...), custom_call_target="tpu_custom_call" | custom-call | tf_op jit(solution)/shard_map/hand_over/pallas_call | solution.py:549

commit v5 on v4

--- a/solution.py
+++ b/solution.py
@@ -80,81 +80,6 @@
         return pl.ds(pl.multiple_of(chip * block, block), block)
 
     come_in[0].wait()
-    pl.semaphore_wait(barrier, outer_size + chip_size - 2)
-
-    def remote(src, dst, send, recv, device):
-        return pltpu.make_async_remote_copy(
-            src_ref=src, dst_ref=dst, send_sem=send, recv_sem=recv, device_id=device, device_id_type=MESH
-        )
-
-    x_partner = (o, 2 * y + 1 - xl)
-
-    def around(steps):
-        return (y + steps + 2 * yn) % yn
-
-    EXPERT = (1, 0, 0)
-    FAR_WAY = (1, -1, 1)
-    WAYS = (1, -1)
-
-    def reach(d, t):
-        return far if d == FAR_WAY[t] else far - 1
-
-    def chip_of(y_at, t):
-        return 2 * y_at + (1 - xl if t == 2 else xl)
-
-    def ag_copy(d, s, t):
-        source = rows(chip_of(around(-d * s), t))
-        k = EXPERT[t]
-        src = hid.at[k] if s == 0 and t < 2 else full.at[k, source]
-        n = WAYS.index(d)
-        return remote(
-            src, full.at[k, source], ag_s.at[n, s, t], ag_r.at[n, s, t], (o, 2 * around(d) + xl)
-        )
-
-    def ag_x(n, k, y_at):
-        source = rows(2 * y_at + xl)
-        src = hid.at[k] if n < 2 else full.at[k, source]
-        return remote(src, full.at[k, source], agx_s.at[n], agx_r.at[n], x_partner)
-
-    def ag_x_of(d, s):
-        return ag_x(2 + WAYS.index(d) * far + s, 1, around(-d * (s + 1)))
-
-    def ag_step(s):
-        for t in range(3):
-            for d in WAYS:
-                if s < reach(d, t):
-                    ag_copy(d, s, t).wait_recv()
-                    if s + 1 < reach(d, t):
-                        ag_copy(d, s + 1, t).start()
-                    if t == 0:
-                        ag_x_of(d, s).start()
-
-    ag_x(0, 0, y).start()
-    for t in range(2):
-        for d in WAYS:
-            if reach(d, t):
-                ag_copy(d, 0, t).start()
-    ag_x(1, 1, y).start()
-
-    def spread(src_of, dst, number, axis_size, device_of):
-        @pl.loop(1, axis_size)
-        def _(i):
-            remote(src_of(i), dst, one_s.at[number], one_r.at[number], device_of(i)).start()
-
-    def arrived(buf, count, number):
-        ref = buf.at[pl.ds(0, count)]
-        pltpu.make_async_copy(ref, ref, one_r.at[number]).wait()
-
-    def sent(buf, count, number):
-        ref = buf.at[pl.ds(0, count)]
-        pltpu.make_async_copy(ref, ref, one_s.at[number]).wait()
-
-    def other_group(i):
-        return (o + i) % outer_size
-
-    def other_chip(i):
-        return (c + i) % chip_size
-
     for copy in come_in[1:5]:
         copy.wait()
     routes_now, gates_now = routes[...], gates[...]
@@ -179,6 +104,82 @@
     outgoing = dot(high, og_now, 1, 0) + dot(low, og_now, 1, 0)
     ob[...] = outgoing.astype(jnp.bfloat16).reshape(ob.shape)
     gb[o] = ob[o]
+
+
+    pl.semaphore_wait(barrier, outer_size + chip_size - 2)
+
+    def remote(src, dst, send, recv, device):
+        return pltpu.make_async_remote_copy(
+            src_ref=src, dst_ref=dst, send_sem=send, recv_sem=recv, device_id=device, device_id_type=MESH
+        )
+
+    x_partner = (o, 2 * y + 1 - xl)
+
+    def around(steps):
+        return (y + steps + 2 * yn) % yn
+
+    EXPERT = (1, 0, 0)
+    FAR_WAY = (1, -1, 1)
+    WAYS = (1, -1)
+
+    def reach(d, t):
+        return far if d == FAR_WAY[t] else far - 1
+
+    def chip_of(y_at, t):
+        return 2 * y_at + (1 - xl if t == 2 else xl)
+
+    def ag_copy(d, s, t):
+        source = rows(chip_of(around(-d * s), t))
+        k = EXPERT[t]
+        src = hid.at[k] if s == 0 and t < 2 else full.at[k, source]
+        n = WAYS.index(d)
+        return remote(
+            src, full.at[k, source], ag_s.at[n, s, t], ag_r.at[n, s, t], (o, 2 * around(d) + xl)
+        )
+
+    def ag_x(n, k, y_at):
+        source = rows(2 * y_at + xl)
+        src = hid.at[k] if n < 2 else full.at[k, source]
+        return remote(src, full.at[k, source], agx_s.at[n], agx_r.at[n], x_partner)
+
+    def ag_x_of(d, s):
+        return ag_x(2 + WAYS.index(d) * far + s, 1, around(-d * (s + 1)))
+
+    def ag_step(s):
+        for t in range(3):
+            for d in WAYS:
+                if s < reach(d, t):
+                    ag_copy(d, s, t).wait_recv()
+                    if s + 1 < reach(d, t):
+                        ag_copy(d, s + 1, t).start()
+                    if t == 0:
+                        ag_x_of(d, s).start()
+
+    ag_x(0, 0, y).start()
+    for t in range(2):
+        for d in WAYS:
+            if reach(d, t):
+                ag_copy(d, 0, t).start()
+    ag_x(1, 1, y).start()
+
+    def spread(src_of, dst, number, axis_size, device_of):
+        @pl.loop(1, axis_size)
+        def _(i):
+            remote(src_of(i), dst, one_s.at[number], one_r.at[number], device_of(i)).start()
+
+    def arrived(buf, count, number):
+        ref = buf.at[pl.ds(0, count)]
+        pltpu.make_async_copy(ref, ref, one_r.at[number]).wait()
+
+    def sent(buf, count, number):
+        ref = buf.at[pl.ds(0, count)]
+        pltpu.make_async_copy(ref, ref, one_s.at[number]).wait()
+
+    def other_group(i):
+        return (o + i) % outer_size
+
+    def other_chip(i):
+        return (c + i) % chip_size
 
     spread(lambda i: ob.at[other_group(i)], gb.at[o], 0, outer_size, lambda i: (other_group(i), c))
 

time: 78.5 us -> 77.9 us (level)
  no operation moved by 1% of the time
where the time goes in v5:
time: 77.9 us; the launch traced here: 77.7 us
  Pallas kernels  77.1 us (99%)
    pallas_call x1, Pallas kernels, on_device(): pl.pallas_call(functools.partial(kernel, (outer_size, chip_size, zn, yn,...  75.3 us
    pallas_call x1, Pallas kernels, on_device(): pl.pallas_call(hand_over, out_shape=results, in_specs=[pl.BlockSpec(memor...  1.74 us

profile of v5, /device:TPU:1, one launch (start us, length us, event | category | flops | bytes accessed | tf_op | source)
XLA Modules:
  0.0 77.7 jit_solution(8536622713714849576)
XLA Ops:
  0.6 75.3 %layer.1 = (bf16[48,448]{1,0:T(8,128)(2,1)}, bf16[2,16,2048]{2,1,0:T(8,128)(2,1)}, f32[2,32,128]{2,1,0:T(8,128)}, f32[2,32,448]{2,1,0:T(8,128)}) custom-call(bf16[2,16,2048]{2,1,0:T(8,128)(2,1)} %hid_in.1, bf16[2,448,2048]{2,1,0:T(8,128)(2,1)} %bitcast.10, bf16[48,448]{1,0:T(8,128)(2,1)} %og_in.1, s32[8,48]{1,0:T(8,128)} %bitcast.15, f32[8,48]{1,0:T(8,128)} %bitcast.16, ...), custom_call_target="tpu_custom_call" | custom-call | tf_op jit(solution)/shard_map/layer/pallas_call | solution.py:499
  76.0 1.7 %hand_over.1 = (bf16[48,448]{1,0:T(8,128)(2,1)}, bf16[2,16,2048]{2,1,0:T(8,128)(2,1)}, f32[2,32,128]{2,1,0:T(8,128)}, f32[2,32,448]{2,1,0:T(8,128)}) custom-call(bf16[48,448]{1,0:T(8,128)(2,1)} %get-tuple-element.12.refs_0_, bf16[2,16,2048]{2,1,0:T(8,128)(2,1)} %get-tuple-element.13.refs_1_, f32[2,32,128]{2,1,0:T(8,128)} %get-tuple-element.14.refs_2_, ...), custom_call_target="tpu_custom_call" | custom-call | tf_op jit(solution)/shard_map/hand_over/pallas_call | solution.py:550
